TPU v7x, 32 devices: a whole 2x2x4 slice. The times are simulated.
32 devices in a mesh: groups: 2 (over y), adapter: 4 (over x, core), tensor: 4 (over z).
Axes of the slice: x: 2, y: 2, z: 4, core: 2. Of those that a mesh axis runs over, the one named last changes fastest.
Arguments:
- normed_hidden: bfloat16 [4096, 4096], P(('groups', 'adapter'), 'tensor'), parts along dimension 0, may hold values from -60 to 60
- query_weight: bfloat16 [4096, 4096], P(None, 'tensor'), may hold values from -0.09375 to 0.09375
- key_value_weight: bfloat16 [2, 4096, 1024], P(None, None, 'tensor'), may hold values from -0.09375 to 0.09375
- output_weight: bfloat16 [4096, 4096], P('tensor'), may hold values from -0.09375 to 0.09375
- adapter_down_rows: bfloat16 [128, 48, 4096], P(('groups', 'adapter')), parts along dimension 0, may hold values from -0.09375 to 0.09375
- adapter_query_up: bfloat16 [128, 16, 4096], P(('groups', 'adapter'), None, 'tensor'), parts along dimension 0, may hold values from -1.5 to 1.5
- adapter_key_value_up: bfloat16 [128, 2, 16, 1024], P(('groups', 'adapter'), None, None, 'tensor'), parts along dimension 0, may hold values from -1.5 to 1.5
- adapter_output_down: bfloat16 [128, 16, 4096], P(('groups', 'adapter'), None, 'tensor'), parts along dimension 0, may hold values from -0.09375 to 0.09375
- adapter_output_up: bfloat16 [128, 16, 4096], P(('groups', 'adapter'), None, 'tensor'), parts along dimension 0, may hold values from -1.5 to 1.5
- adapter_cache_row: int32 [128], P('groups'), parts along dimension 0, may hold values from 0 to 63, as said below
- request_adapter_index: int32 [8, 4], P(('groups', 'adapter')), parts along dimension 0, may hold values from 0 to 63, as said below
- request_token_length: int32 [8, 4], P(('groups', 'adapter')), parts along dimension 0, may hold values from 1 to 256, 512 in all within a row
Outputs:
- mixed: bfloat16 [4096, 4096], P(('groups', 'adapter'), 'tensor'), parts along dimension 0
- kv_cache: bfloat16 [2, 4096, 1024], P(None, ('groups', 'adapter'), 'tensor'), parts along dimension 1
There are 2 independent parts, one for each index of `groups`. A program takes and returns all parts, laid end to end along the dimension named above; an argument that names none is the same for every part. Nothing has to cross between parts.
Inputs may be any that keep to these rules, and one draw needn't show every extreme that they name: `adapter_cache_row`: a permutation of the cache rows. `request_adapter_index`: in each row, at most 2 requests name adapters whose adapter_cache_row values lie in one aligned block of 16 values, and in every row some block holds exactly 2. `request_token_length`: each row sums to 512.
All inputs are finite; a program needn't handle non-finite values.
Results may differ from a plain program's by a relative error of at most 0.012.
The roundings to bfloat16 on the way count: a program that leaves them out, or rounds other values in their place, can miss the bound.
Values may be sent and summed in bfloat16 or wider, within the bound.
A program may use at most 128 MiB of HBM per device.

v0:
```python
import jax
import jax.numpy as jnp
from jax import lax
from jax.sharding import PartitionSpec as P

HEAD_WIDTH = 128
CAP = 2


SCORE_SCALE = 0.5
THETA = 500000.0
NEG_FILL = -1e30


def apply_rotation(values, token_position):
    half_width = values.shape[-1] // 2
    exponent = jnp.arange(half_width).astype(jnp.float32) * (2.0 / values.shape[-1])
    frequency = THETA ** (-exponent)
    angles = token_position.astype(jnp.float32)[:, None] * frequency[None, :]
    cosine = jnp.cos(angles)[:, None, :]
    sine_part = jnp.sin(angles)[:, None, :]
    front_part = values[..., :half_width]
    back_part = values[..., half_width:]
    return jnp.concatenate(
        [front_part * cosine - back_part * sine_part, back_part * cosine + front_part * sine_part],
        axis=-1,
    )


def request_layout(lengths, token_count):
    ending = jnp.cumsum(lengths)
    starting = ending - lengths
    token_index = jnp.arange(token_count, dtype=jnp.int32)
    segment = jnp.sum((token_index[:, None] >= ending[None, :]).astype(jnp.int32), axis=1)
    member = segment[:, None] == jnp.arange(lengths.shape[0], dtype=jnp.int32)[None, :]
    token_position = token_index - jnp.sum(jnp.where(member, starting[None, :], 0), axis=1)
    return (segment, token_position, member)


def local(
    normed_hidden,
    query_weight,
    key_value_weight,
    output_weight,
    adapter_down_rows,
    adapter_query_up,
    adapter_key_value_up,
    adapter_output_down,
    adapter_output_up,
    adapter_cache_row,
    request_adapter_index,
    request_token_length,
):
    token_count = normed_hidden.shape[0]
    slice_width = normed_hidden.shape[1]
    adapter_rank_width = adapter_query_up.shape[1]
    held_adapter_count = adapter_down_rows.shape[0]
    owner_count = lax.axis_size("adapter")
    query_cols = query_weight.shape[1]
    keyval_cols = key_value_weight.shape[2]
    request_ids = request_adapter_index[0]
    lengths = request_token_length[0]
    request_count = request_ids.shape[0]
    catalog = jnp.arange(adapter_cache_row.shape[0], dtype=jnp.int32)
    holder_rows = jnp.sum(
        jnp.where(request_ids[:, None] == catalog[None, :], adapter_cache_row[None, :], 0), axis=1
    )
    owner_index = holder_rows // held_adapter_count
    local_slot = holder_rows % held_adapter_count
    request_order = jnp.arange(request_count, dtype=jnp.int32)
    earlier = (owner_index[:, None] == owner_index[None, :]) & (
        request_order[None, :] < request_order[:, None]
    )
    rank_within = jnp.sum(earlier.astype(jnp.int32), axis=1)
    placed = owner_index * CAP + rank_within
    targets = jnp.arange(owner_count * CAP, dtype=jnp.int32)
    want_table = (
        jnp.sum(jnp.where(placed[:, None] == targets[None, :], local_slot[:, None] + 1, 0), axis=0)
        - 1
    )
    want_table = want_table.reshape(owner_count, CAP)
    wanted = lax.all_to_all(want_table, "adapter", split_axis=0, concat_axis=0, tiled=True)
    is_valid = wanted >= 0
    picked = jnp.maximum(wanted, 0)

    def select_rows(stored):
        chosen = jnp.take(stored, picked, axis=0)
        keep_mask = is_valid.reshape(is_valid.shape + (1,) * (chosen.ndim - 2))
        return jnp.where(keep_mask, chosen, jnp.zeros((), stored.dtype))

    fetched = (
        lax.all_to_all(
            select_rows(adapter_down_rows), "adapter", split_axis=0, concat_axis=0, tiled=True
        ),
        lax.all_to_all(
            select_rows(adapter_query_up), "adapter", split_axis=0, concat_axis=0, tiled=True
        ),
        lax.all_to_all(
            select_rows(adapter_key_value_up), "adapter", split_axis=0, concat_axis=0, tiled=True
        ),
        lax.all_to_all(
            select_rows(adapter_output_down), "adapter", split_axis=0, concat_axis=0, tiled=True
        ),
        lax.all_to_all(
            select_rows(adapter_output_up), "adapter", split_axis=0, concat_axis=0, tiled=True
        ),
    )
    slot_total = owner_count * CAP
    req_down, req_qup, req_kvup, req_odown, req_oup = [
        jnp.take(received.reshape((slot_total,) + received.shape[2:]), placed, axis=0)
        for received in fetched
    ]
    segment, token_position, member = request_layout(lengths, token_count)
    member_low = member.astype(jnp.bfloat16)

    def spread(low_part):
        return (member_low[:, :, None] * low_part[:, None, :]).reshape(
            token_count, request_count * adapter_rank_width
        )

    gathered = lax.all_gather(normed_hidden, "tensor", axis=1, tiled=True)
    low_next = jnp.einsum("td,jrd->tjr", gathered, req_down, preferred_element_type=jnp.float32)
    base_query = jnp.dot(gathered, query_weight, preferred_element_type=jnp.float32)
    base_keyval = jnp.einsum(
        "td,sdc->stc", gathered, key_value_weight, preferred_element_type=jnp.float32
    )
    low_in = jnp.sum(jnp.where(member[:, :, None], low_next, 0.0), axis=1).astype(jnp.bfloat16)
    flat_rank = request_count * adapter_rank_width
    query_lin = base_query + SCORE_SCALE * jnp.dot(
        spread(low_in[:, 0:adapter_rank_width]),
        req_qup.reshape(flat_rank, query_cols),
        preferred_element_type=jnp.float32,
    )
    key_linear = base_keyval[0] + SCORE_SCALE * jnp.dot(
        spread(low_in[:, adapter_rank_width : 2 * adapter_rank_width]),
        req_kvup[:, 0].reshape(flat_rank, keyval_cols),
        preferred_element_type=jnp.float32,
    )
    value_linear = base_keyval[1] + SCORE_SCALE * jnp.dot(
        spread(low_in[:, 2 * adapter_rank_width : 3 * adapter_rank_width]),
        req_kvup[:, 1].reshape(flat_rank, keyval_cols),
        preferred_element_type=jnp.float32,
    )
    query_local = query_cols // HEAD_WIDTH
    keyval_local = keyval_cols // HEAD_WIDTH
    query_group_width = query_local // keyval_local
    query_head_rows = apply_rotation(
        query_lin.reshape(token_count, query_local, HEAD_WIDTH), token_position
    ).astype(jnp.bfloat16)
    key_head_rows = apply_rotation(
        key_linear.reshape(token_count, keyval_local, HEAD_WIDTH), token_position
    ).astype(jnp.bfloat16)
    value_head_rows = value_linear.astype(jnp.bfloat16).reshape(
        token_count, keyval_local, HEAD_WIDTH
    )
    kv_cache = jnp.stack(
        [
            key_head_rows.reshape(token_count, keyval_cols),
            value_head_rows.reshape(token_count, keyval_cols),
        ],
        axis=0,
    )
    token_index = jnp.arange(token_count, dtype=jnp.int32)
    allowed = (segment[:, None] == segment[None, :]) & (
        token_index[None, :] <= token_index[:, None]
    )
    attention_scores = jnp.einsum(
        "hoyr,lor->oyhl",
        query_head_rows.reshape(token_count, keyval_local, query_group_width, HEAD_WIDTH),
        key_head_rows,
        preferred_element_type=jnp.float32,
    ) * HEAD_WIDTH ** (-0.5)
    attention_scores = jnp.where(allowed[None, None], attention_scores, NEG_FILL)
    maximum = jnp.max(attention_scores, axis=-1, keepdims=True)
    exponent_part = jnp.exp(attention_scores - maximum)
    weights = (exponent_part / jnp.sum(exponent_part, axis=-1, keepdims=True)).astype(jnp.bfloat16)
    attended = (
        jnp.einsum("kgts,skd->tkgd", weights, value_head_rows, preferred_element_type=jnp.float32)
        .reshape(token_count, query_cols)
        .astype(jnp.bfloat16)
    )
    partial_out = jnp.einsum("tc,jrc->tjr", attended, req_odown, preferred_element_type=jnp.float32)
    picked_out = jnp.sum(jnp.where(member[:, :, None], partial_out, 0.0), axis=1)
    low_out = lax.psum(picked_out, "tensor").astype(jnp.bfloat16)
    adapter_term = jnp.dot(
        spread(low_out), req_oup.reshape(flat_rank, slice_width), preferred_element_type=jnp.float32
    )
    base_output = lax.psum_scatter(
        jnp.dot(attended, output_weight, preferred_element_type=jnp.float32),
        "tensor",
        scatter_dimension=1,
        tiled=True,
    )
    mixed = (base_output + SCORE_SCALE * adapter_term).astype(jnp.bfloat16)
    return (mixed, kv_cache)


def solution(mesh):
    in_specs = (
        P(("groups", "adapter"), "tensor"),
        P(None, "tensor"),
        P(None, None, "tensor"),
        P("tensor", None),
        P(("groups", "adapter"), None, None),
        P(("groups", "adapter"), None, "tensor"),
        P(("groups", "adapter"), None, None, "tensor"),
        P(("groups", "adapter"), None, "tensor"),
        P(("groups", "adapter"), None, "tensor"),
        P("groups"),
        P(("groups", "adapter"), None),
        P(("groups", "adapter"), None),
    )
    out_specs = (P(("groups", "adapter"), "tensor"), P(None, ("groups", "adapter"), "tensor"))
    return jax.shard_map(local, mesh=mesh, in_specs=in_specs, out_specs=out_specs, check_vma=False)
```

profile of v0, /device:TPU:0, one launch (start us, length us, event | category | flops | bytes accessed | tf_op | source)
XLA Modules:
  0.0 288.1 jit_solution(17995098593822874913)
XLA Ops:
  7.2 0.7 all-gather.2.cloned.1.call-update
  7.9 0.9 select_reduce_fusion.2
  10.2 0.7 sub.38
  10.9 4.2 %all-to-all-start = ((s32[4,1,2]{2,1,0:T(1,128)}), s32[4,1,2]{2,1,0:T(1,128)S(1)}, u32[]{:S(2)}, u32[]{:S(2)}) async-start(s32[4,1,2]{2,1,0:T(1,128)} %bitcast.6), calls=%async_computation | async-start | bytes 4096 | tf_op jit(solution)/shard_map/all_to_all | solution.py:82
  15.1 0.8 reduce-window.4
  16.5 2.3 all-to-all-done
  19.4 1.5 gather_fusion.2
  20.9 0.7 select_select_fusion.4
  21.7 3.3 %all-to-all-start.2 = ((bf16[4,2,2,16,256]{4,3,2,1,0:T(8,128)(2,1)}), bf16[4,2,2,16,256]{4,3,2,1,0:T(8,128)(2,1)S(1)}, u32[]{:S(2)}, u32[]{:S(2)}) async-start(bf16[4,2,2,16,256]{4,3,2,1,0:T(8,128)(2,1)} %select_select_fusion.4), calls=%async_computation.2 | async-start | bytes 262144 | tf_op jit(solution)/shard_map/all_to_all | solution.py:98
  25.6 1.6 gather_fusion.6
  27.8 1.0 select_select_fusion.2
  28.8 3.5 %gather_fusion = bf16[8,48,4096]{2,1,0:T(8,128)(2,1)S(1)} fusion(bf16[16,48,4096]{2,1,0:T(8,128)(2,1)} %param.20, s32[1024]{0:T(1024)S(1)} %pad_clamp_fusion.3), kind=kCustom, calls=%fused_computation.6 | custom fusion | bytes 6291488 | tf_op jit(solution)/shard_map/jit(_take)/gather | solution.py:87
  32.3 3.4 %all-to-all-start.3 = ((bf16[4,2,16,1024]{3,2,1,0:T(8,128)(2,1)}), bf16[4,2,16,1024]{3,2,1,0:T(8,128)(2,1)S(1)}, u32[]{:S(2)}, u32[]{:S(2)}) async-start(bf16[4,2,16,1024]{3,2,1,0:T(8,128)(2,1)} %get-tuple-element.37), calls=%async_computation.3 | async-start | bytes 524288 | tf_op jit(solution)/shard_map/all_to_all | solution.py:95
  35.8 2.1 select_select_fusion
  37.9 3.9 %all-to-all-done.3 = bf16[4,2,16,1024]{3,2,1,0:T(8,128)(2,1)S(1)} async-done(((bf16[4,2,16,1024]{3,2,1,0:T(8,128)(2,1)}), bf16[4,2,16,1024]{3,2,1,0:T(8,128)(2,1)S(1)}, u32[]{:S(2)}, u32[]{:S(2)}) %all-to-all-start.3) | async-done | bytes 262176 | tf_op jit(solution)/shard_map/all_to_all | solution.py:95
  41.8 0.7 copy-done.6
  42.5 3.7 %all-to-all-start.1 = ((bf16[4,2,48,4096]{3,2,1,0:T(8,128)(2,1)}), bf16[4,2,48,4096]{3,2,1,0:T(8,128)(2,1)S(1)}, u32[]{:S(2)}, u32[]{:S(2)}) async-start(bf16[4,2,48,4096]{3,2,1,0:T(8,128)(2,1)} %select_select_fusion), calls=%async_computation.1 | async-start | bytes 6291456 | tf_op jit(solution)/shard_map/all_to_all | solution.py:92
  46.2 0.7 fusion.63
  47.8 1.1 compare_and_fusion.1
  48.9 0.9 fusion.43
  49.8 2.4 multiply_cosine_fusion
  52.2 1.2 gather_fusion.3
  53.3 0.9 broadcast_select_fusion
  54.9 1.5 gather_fusion.5
  56.4 26.7 %all-to-all-done.1 = bf16[4,2,48,4096]{3,2,1,0:T(8,128)(2,1)S(1)} async-done(((bf16[4,2,48,4096]{3,2,1,0:T(8,128)(2,1)}), bf16[4,2,48,4096]{3,2,1,0:T(8,128)(2,1)S(1)}, u32[]{:S(2)}, u32[]{:S(2)}) %all-to-all-start.1) | async-done | bytes 3145760 | tf_op jit(solution)/shard_map/all_to_all | solution.py:92
  83.1 1.8 gather_fusion.1
  84.9 8.2 %all-gather.2.cloned.1.call-done = bf16[512,4096]{1,0:T(8,128)(2,1)} async-done(((bf16[512,1024]{1,0:T(8,128)(2,1)}), bf16[512,4096]{1,0:T(8,128)(2,1)}) %all-gather.2.cloned.1.call-update) | async-done | bytes 4194320 | tf_op jit(solution)/shard_map/all_gather | solution.py:121
  93.1 4.4 %fusion.33 = bf16[512,48]{0,1:T(8,128)(2,1)S(1)} fusion(bf16[512,4096]{1,0:T(8,128)(2,1)} %all-gather.2.cloned.1.call-done, bf16[4,48,4096]{2,1,0:T(8,128)(2,1)} %gather_fusion.1, pred[4]{0:T(512)(128)(4,1)} %compare_and_fusion.1, pred[512,4]{0,1:T(4,128)(4,1)S(1)} %get-tuple-element.32), kind=kOutput, calls=%fused_computation.43 | convolution fusion | flops 806264832 | bytes 5818372 | tf_op jit(solution)/shard_map/td,jrd->tjr/dot_general | solution.py:122
  97.5 6.9 %fusion.78 = f32[512,1024]{1,0:T(8,128)S(1)} fusion(bf16[512,4096]{1,0:T(8,128)(2,1)S(1)} %copy-done.16, bf16[4096,1024]{1,0:T(8,128)(2,1)} %param.17), kind=kOutput, calls=%fused_computation.140 | convolution fusion | flops 4294967296 | bytes 14680064 | tf_op jit(solution)/shard_map/dot_general | solution.py:123
  105.9 0.9 subtract_convert_fusion
  106.9 1.2 copy-done.15
  108.1 2.4 fusion.17
  110.8 0.8 fusion.74
  111.6 1.1 copy.115
  112.7 1.0 copy.114
  113.9 1.3 fusion.22
  115.5 1.3 fusion.39
  116.9 5.7 %fusion.77 = (f32[2,4,512]{2,1,0:T(4,128)S(1)}, f32[2,4,512,512]{2,3,1,0:T(8,128)}) fusion(f32[2,512,512,4]{2,1,3,0:T(8,128)S(1)} %fusion.39, pred[512,512]{0,1:T(8,128)(4,1)S(1)} %copy-done.7), kind=kOutput, calls=%fused_computation.139 | output fusion | flops 12583423 | bytes 17055744 | tf_op jit(solution)/shard_map/sub | solution.py:175
  122.6 4.3 %fusion.16 = bf16[2,128,4,512]{3,1,2,0:T(8,128)(2,1)S(1)} fusion(bf16[512,2,128,1]{0,2,3,1:T(8,128)(2,1)S(1)} %bitcast.144, f32[2,4,512,512]{2,3,1,0:T(8,128)} %get-tuple-element.43, f32[2,4,512]{2,1,0:T(4,128)S(1)} %get-tuple-element.42), kind=kOutput, calls=%fused_computation.34 | convolution fusion | flops 541589504 | bytes 9715712 | tf_op jit(solution)/shard_map/kgts,skd->tkgd/dot_general | solution.py:178
  127.2 6.9 %fusion.79 = f32[512,4096]{1,0:T(8,128)} fusion(bf16[512,1024]{0,1:T(8,128)(2,1)S(1)} %bitcast.142, bf16[1024,4096]{1,0:T(8,128)(2,1)S(1)} %bitcast.137), kind=kOutput, calls=%fused_computation.141 | convolution fusion | flops 4294967296 | bytes 17825792 | tf_op jit(solution)/shard_map/dot_general | solution.py:189
  134.0 0.9 copy-done.5
  135.0 8.6 %all_to_all.31 = bf16[4,2,16,1024]{3,2,1,0:T(8,128)(2,1)S(1)} all-to-all(bf16[4,2,16,1024]{3,2,1,0:T(8,128)(2,1)S(1)} %copy-done.5), channel_id=1, replica_groups=mesh['groups'=2,'adapter'=4,'tensor'=4] {'adapter'}, dimensions={0} | all-to-all | bytes 524288 | tf_op jit(solution)/shard_map/all_to_all | solution.py:101
  143.5 3.4 %all-to-all-start.5 = ((bf16[4,2,16,1024]{3,2,1,0:T(8,128)(2,1)}), bf16[4,2,16,1024]{3,2,1,0:T(8,128)(2,1)S(1)}, u32[]{:S(2)}, u32[]{:S(2)}) async-start(bf16[4,2,16,1024]{3,2,1,0:T(8,128)(2,1)} %get-tuple-element.36), calls=%async_computation.6 | async-start | bytes 524288 | tf_op jit(solution)/shard_map/all_to_all | solution.py:104
  147.5 5.4 %all-to-all-done.5 = bf16[4,2,16,1024]{3,2,1,0:T(8,128)(2,1)S(1)} async-done(((bf16[4,2,16,1024]{3,2,1,0:T(8,128)(2,1)}), bf16[4,2,16,1024]{3,2,1,0:T(8,128)(2,1)S(1)}, u32[]{:S(2)}, u32[]{:S(2)}) %all-to-all-start.5) | async-done | bytes 262176 | tf_op jit(solution)/shard_map/all_to_all | solution.py:104
  153.7 1.0 copy.106
  155.1 18.0 %psum.7 = bf16[512,16]{0,1:T(8,128)(2,1)S(1)} all-reduce(f32[512,16]{0,1:T(8,128)S(1)} %fusion.38), channel_id=1, replica_groups=mesh['groups'=2,'adapter'=4,'tensor'=4] {'tensor'}, use_global_device_ids=true, to_apply=%region_11.14 | all-reduce | flops 8192 | bytes 49152 | tf_op jit(solution)/shard_map/psum | solution.py:184
  173.1 105.1 %reduce-scatter.2.cloned.1.call-done = f32[512,1024]{1,0:T(8,128)} async-done(((f32[512,4096]{1,0:T(8,128)}), f32[512,1024]{1,0:T(8,128)}) %reduce-scatter.2.cloned.1.call-update) | async-done | bytes 2097168 | tf_op jit(solution)/shard_map/reduce_scatter | solution.py:188
  278.2 3.0 %fusion.11 = bf16[512,1024]{1,0:T(8,128)(2,1)} fusion(f32[512,1024]{1,0:T(8,128)} %reduce-scatter.2.cloned.1.call-done, bf16[4,16,1024]{2,1,0:T(8,128)(2,1)S(1)} %gather_fusion.9, pred[4]{0:T(512)(128)(4,1)S(1)} %copy-done.11, bf16[512,16]{0,1:T(8,128)(2,1)S(1)} %psum.7, bf16[512,4]{0,1:T(4,128)(2,1)S(1)} %get-tuple-element.31), kind=kOutput, calls=%fused_computation.26 | convolution fusion | flops 68780032 | bytes 3297284 | tf_op jit(solution)/shard_map/dot_general | solution.py:185
  (85 shorter events, 9.6 us)
Async XLA Ops:
  7.2 17.9 %copy-start = (bf16[16,16,1024]{2,1,0:T(8,128)(2,1)S(1)}, bf16[16,16,1024]{2,1,0:T(8,128)(2,1)}, u32[]{:S(2)}) copy-start(bf16[16,16,1024]{2,1,0:T(8,128)(2,1)} %param.24) | copy-start | bytes 1572868
  7.2 20.0 %copy-start.9 = (bf16[16,16,1024]{2,1,0:T(8,128)(2,1)S(1)}, bf16[16,16,1024]{2,1,0:T(8,128)(2,1)}, u32[]{:S(2)}) copy-start(bf16[16,16,1024]{2,1,0:T(8,128)(2,1)} %param.21) | copy-start | bytes 1572868
  7.2 85.9 %all-gather.2.cloned.1.call-start = ((), (), s32[]{:S(2)}) async-start(), calls=%async_computation.7 | async-start | bytes 5242880 | tf_op jit(solution)/shard_map/all_gather | solution.py:121
  8.8 0.6 copy-start.17
  9.6 9.2 %copy-start.13 = (s32[4]{0:T(128)}, s32[4]{0:T(128)S(1)}, u32[]{:S(2)}) copy-start(s32[4]{0:T(128)S(1)} %convert_reduce_fusion.1) | copy-start | bytes 52
  9.6 0.5 copy-start.12
  10.9 7.9 %all-to-all-start = ((s32[4,1,2]{2,1,0:T(1,128)}), s32[4,1,2]{2,1,0:T(1,128)S(1)}, u32[]{:S(2)}, u32[]{:S(2)}) async-start(s32[4,1,2]{2,1,0:T(1,128)} %bitcast.6), calls=%async_computation | async-start | bytes 4096 | tf_op jit(solution)/shard_map/all_to_all | solution.py:82
  21.7 10.6 %all-to-all-start.2 = ((bf16[4,2,2,16,256]{4,3,2,1,0:T(8,128)(2,1)}), bf16[4,2,2,16,256]{4,3,2,1,0:T(8,128)(2,1)S(1)}, u32[]{:S(2)}, u32[]{:S(2)}) async-start(bf16[4,2,2,16,256]{4,3,2,1,0:T(8,128)(2,1)} %select_select_fusion.4), calls=%async_computation.2 | async-start | bytes 262144 | tf_op jit(solution)/shard_map/all_to_all | solution.py:98
  32.3 9.4 %all-to-all-start.3 = ((bf16[4,2,16,1024]{3,2,1,0:T(8,128)(2,1)}), bf16[4,2,16,1024]{3,2,1,0:T(8,128)(2,1)S(1)}, u32[]{:S(2)}, u32[]{:S(2)}) async-start(bf16[4,2,16,1024]{3,2,1,0:T(8,128)(2,1)} %get-tuple-element.37), calls=%async_computation.3 | async-start | bytes 524288 | tf_op jit(solution)/shard_map/all_to_all | solution.py:95
  37.8 8.4 %copy-start.14 = (s32[4]{0:T(128)S(1)}, s32[4]{0:T(128)}, u32[]{:S(2)}) copy-start(s32[4]{0:T(128)} %copy-done.13) | copy-start | bytes 52
  41.8 0.7 copy-start.6
  42.5 40.6 %all-to-all-start.1 = ((bf16[4,2,48,4096]{3,2,1,0:T(8,128)(2,1)}), bf16[4,2,48,4096]{3,2,1,0:T(8,128)(2,1)S(1)}, u32[]{:S(2)}, u32[]{:S(2)}) async-start(bf16[4,2,48,4096]{3,2,1,0:T(8,128)(2,1)} %select_select_fusion), calls=%async_computation.1 | async-start | bytes 6291456 | tf_op jit(solution)/shard_map/all_to_all | solution.py:92
  46.2 232.0 %reduce-scatter.2.cloned.1.call-start = ((), (), s32[]{:S(2)}) async-start(), calls=%async_computation.8 | async-start | bytes 10485760 | tf_op jit(solution)/shard_map/reduce_scatter | solution.py:188
  93.1 4.4 %copy-start.16 = (bf16[512,4096]{1,0:T(8,128)(2,1)S(1)}, bf16[512,4096]{1,0:T(8,128)(2,1)}, u32[]{:S(2)}) copy-start(bf16[512,4096]{1,0:T(8,128)(2,1)} %all-gather.2.cloned.1.call-done) | copy-start | bytes 12582916
  97.5 7.0 %copy-start.11 = (pred[4]{0:T(512)(128)(4,1)S(1)}, pred[4]{0:T(512)(128)(4,1)}, u32[]{:S(2)}) copy-start(pred[4]{0:T(512)(128)(4,1)} %compare_and_fusion.1) | copy-start | bytes 16
  105.0 1.0 copy-start.2
  105.9 2.2 copy-start.15
  108.1 2.4 copy-start.10
  110.5 1.1 copy-start.4
  110.5 3.4 %copy-start.8 = (bf16[4,1,16,256]{3,2,1,0:T(8,128)(2,1)S(1)}, bf16[4,1,16,256]{3,2,1,0:T(8,128)(2,1)}, u32[]{:S(2)}) copy-start(bf16[4,1,16,256]{3,2,1,0:T(8,128)(2,1)} %get-tuple-element.23) | copy-start | bytes 98308
  113.7 1.5 copy-start.3
  115.5 1.4 copy-start.7
  116.9 10.0 %slice-start = ((s8[8388608]{0:T(1024)(128)(4,1)}), s8[4194304]{0:T(1024)(128)(4,1)S(1)}, s32[]{:S(2)}) async-start(s8[8388608]{0:T(1024)(128)(4,1)} %bitcast.136), calls=%async_computation.9 | async-start | bytes 8388608
  122.6 4.6 %slice-start.1 = ((s8[8388608]{0:T(1024)(128)(4,1)}), s8[4194304]{0:T(1024)(128)(4,1)S(1)}, s32[]{:S(2)}) async-start(s8[8388608]{0:T(1024)(128)(4,1)} %bitcast.136), calls=%async_computation.10 | async-start | bytes 8388608
  134.0 0.9 copy-start.5
  143.5 9.4 %all-to-all-start.5 = ((bf16[4,2,16,1024]{3,2,1,0:T(8,128)(2,1)}), bf16[4,2,16,1024]{3,2,1,0:T(8,128)(2,1)S(1)}, u32[]{:S(2)}, u32[]{:S(2)}) async-start(bf16[4,2,16,1024]{3,2,1,0:T(8,128)(2,1)} %get-tuple-element.36), calls=%async_computation.6 | async-start | bytes 524288 | tf_op jit(solution)/shard_map/all_to_all | solution.py:104
  154.7 126.6 %copy-start.1 = (bf16[16,16,1024]{2,1,0:T(8,128)(2,1)S(1)}, bf16[16,16,1024]{2,1,0:T(8,128)(2,1)}, u32[]{:S(2)}) copy-start(bf16[16,16,1024]{2,1,0:T(8,128)(2,1)} %param.24) | copy-start | bytes 1572868
Sparse Core Ops, SparseCore 0:
  9.6 83.4 all-gather.1
  134.2 144.0 reduce-scatter.1
where the time goes:
time: 289 us; the launch traced here: 288 us
  waiting for transfers between devices  152 us (53%)
  matrix products  31.6 us (11%)
  blocking collectives  26.6 us (9%)
  local copies, waits for them, and re-layouts  24.8 us (9%)
  other arithmetic  20.1 us (7%)
  starting transfers between devices  18.1 us (6%)
  between operations  14.5 us (5%)
    reduce_scatter x1, waiting for transfers between devices, local(): lax.psum_scatter(jnp.dot(attended, output_weight, preferred_element_type=...  105 us
    all_to_all x1, waiting for transfers between devices, local(): lax.all_to_all(select_rows(adapter_down_rows), 'adapter', split_axis=0, c...  26.7 us
    psum x1, blocking collectives, local(): low_out = lax.psum(picked_out, 'tensor').astype(jnp.bfloat16)  18 us
    all_to_all x1, blocking collectives, local(): lax.all_to_all(select_rows(adapter_output_down), 'adapter', split_axis=0,...  8.55 us
    unnamed x45, local copies, waits for them, and re-layouts  8.34 us
    all_gather x1, waiting for transfers between devices, local(): gathered = lax.all_gather(normed_hidden, 'tensor', axis=1, tiled=True)  8.19 us
    gather x5, local copies, waits for them, and re-layouts, select_rows(): chosen = jnp.take(stored, picked, axis=0)  7.8 us
    dot_general x1, matrix products, local(): jnp.dot(gathered, query_weight, preferred_element_type=jnp.float32)  6.94 us
  transfers between devices with their start and end apart: 7, of which 6 were waited for; matrix products, arithmetic and copies ran while one was open for 10% of the time, Pallas kernels for 0%

commit v1 on v0

v1 whole, which is shorter than its diff:
```python
import jax
import jax.numpy as jnp
from jax import lax
from jax.sharding import PartitionSpec as P

HEAD_WIDTH = 128
CAP = 2
CHUNKS = 2


SCORE_SCALE = 0.5
THETA = 500000.0
NEG_FILL = -1e30


def rotation_tables(token_position):
    half_width = HEAD_WIDTH // 2
    exponent = jnp.arange(half_width).astype(jnp.float32) * (2.0 / HEAD_WIDTH)
    frequency = THETA ** (-exponent)
    angles = token_position.astype(jnp.float32)[:, None] * frequency[None, :]
    return jnp.cos(angles)[:, None, :], jnp.sin(angles)[:, None, :]


def apply_rotation(values, cosine, sine_part):
    half_width = values.shape[-1] // 2
    front_part = values[..., :half_width]
    back_part = values[..., half_width:]
    return jnp.concatenate(
        [front_part * cosine - back_part * sine_part, back_part * cosine + front_part * sine_part],
        axis=-1,
    )


def request_layout(lengths, token_count):
    ending = jnp.cumsum(lengths)
    starting = ending - lengths
    token_index = jnp.arange(token_count, dtype=jnp.int32)
    segment = jnp.sum((token_index[:, None] >= ending[None, :]).astype(jnp.int32), axis=1)
    member = segment[:, None] == jnp.arange(lengths.shape[0], dtype=jnp.int32)[None, :]
    token_position = token_index - jnp.sum(jnp.where(member, starting[None, :], 0), axis=1)
    return (segment, token_position, member)


def after(value, *others):
    return lax.optimization_barrier((value,) + others)[0]


def line_gather(own, me, count, previous):
    width = own.shape[1]
    right = left = own if previous is None else after(own, *previous)
    from_left, from_right, marks = [None], [None], []
    for step in range(1, count):
        right = lax.ppermute(right, "tensor", [(i, i + 1) for i in range(step - 1, count - 1)])
        left = lax.ppermute(left, "tensor", [(i, i - 1) for i in range(1, count - step + 1)])
        from_left.append(right)
        from_right.append(left)
        if step == max(1, count - 2):
            marks = (right, left)
    whole = jnp.zeros((own.shape[0], width * count), own.dtype)
    whole = lax.dynamic_update_slice(whole, own, (0, me * width))
    for k in range(1, count):
        block = jnp.where(me + k < count, from_right[k], from_left[count - k])
        whole = lax.dynamic_update_slice(whole, block, (0, ((me + k) % count) * width))
    return whole, marks


def line_reduce(partial, me, count):
    width = partial.shape[1] // count

    def block(index):
        return lax.dynamic_slice(partial, (0, index * width), (partial.shape[0], width))

    right = left = None
    for step in range(1, count):
        to_right = block((me + count - step) % count)
        to_left = block((me + step) % count)
        if right is not None:
            to_right = to_right + right.astype(jnp.float32)
            to_left = to_left + left.astype(jnp.float32)
        right = lax.ppermute(
            to_right.astype(jnp.bfloat16), "tensor", [(i, i + 1) for i in range(min(step, count - 1))]
        )
        left = lax.ppermute(
            to_left.astype(jnp.bfloat16), "tensor", [(i, i - 1) for i in range(count - step, count)]
        )
    return block(me) + right.astype(jnp.float32) + left.astype(jnp.float32)


def small_sum(own, count):
    total = own
    for k in range(1, count):
        total = total + lax.ppermute(own, "tensor", [(i, (i + k) % count) for i in range(count)])
    return total


def local(
    normed_hidden,
    query_weight,
    key_value_weight,
    output_weight,
    adapter_down_rows,
    adapter_query_up,
    adapter_key_value_up,
    adapter_output_down,
    adapter_output_up,
    adapter_cache_row,
    request_adapter_index,
    request_token_length,
):
    token_count = normed_hidden.shape[0]
    slice_width = normed_hidden.shape[1]
    rank = adapter_query_up.shape[1]
    held_adapter_count = adapter_down_rows.shape[0]
    owner_count = lax.axis_size("adapter")
    count = lax.axis_size("tensor")
    me = lax.axis_index("tensor")
    query_cols = query_weight.shape[1]
    keyval_cols = key_value_weight.shape[2]
    query_local = query_cols // HEAD_WIDTH
    keyval_local = keyval_cols // HEAD_WIDTH
    query_group_width = query_local // keyval_local
    size = token_count // CHUNKS

    gathered, marks = [], None
    for c in range(CHUNKS):
        whole, marks = line_gather(normed_hidden[c * size : (c + 1) * size], me, count, marks)
        gathered.append(whole)

    request_ids = request_adapter_index[0]
    lengths = request_token_length[0]
    request_count = request_ids.shape[0]
    catalog = jnp.arange(adapter_cache_row.shape[0], dtype=jnp.int32)
    holder_rows = jnp.sum(
        jnp.where(request_ids[:, None] == catalog[None, :], adapter_cache_row[None, :], 0), axis=1
    )
    owner_index = holder_rows // held_adapter_count
    local_slot = holder_rows % held_adapter_count
    request_order = jnp.arange(request_count, dtype=jnp.int32)
    earlier = (owner_index[:, None] == owner_index[None, :]) & (
        request_order[None, :] < request_order[:, None]
    )
    rank_within = jnp.sum(earlier.astype(jnp.int32), axis=1)
    placed = owner_index * CAP + rank_within
    targets = jnp.arange(owner_count * CAP, dtype=jnp.int32)
    want_table = jnp.sum(
        jnp.where(placed[:, None] == targets[None, :], local_slot[:, None], 0), axis=0
    )
    want_table = want_table.reshape(owner_count, CAP)
    picked = lax.all_to_all(want_table, "adapter", split_axis=0, concat_axis=0, tiled=True)

    def fetch(rows):
        received = lax.all_to_all(rows, "adapter", split_axis=0, concat_axis=0, tiled=True)
        received = received.reshape((owner_count * CAP,) + rows.shape[2:])
        return jnp.take(received, placed, axis=0)

    req_down = fetch(jnp.take(adapter_down_rows, picked, axis=0))
    small = fetch(
        jnp.concatenate(
            [
                jnp.take(adapter_query_up, picked, axis=0),
                jnp.take(adapter_key_value_up[:, 0], picked, axis=0),
                jnp.take(adapter_key_value_up[:, 1], picked, axis=0),
                jnp.take(adapter_output_down, picked, axis=0),
                jnp.take(adapter_output_up, picked, axis=0),
            ],
            axis=-1,
        )
    )
    flat_rank = request_count * rank
    cuts, at = [], 0
    for width in (query_cols, keyval_cols, keyval_cols, query_cols, slice_width):
        cuts.append(small[:, :, at : at + width].reshape(flat_rank, width))
        at += width
    query_up, key_up, value_up, out_down, out_up = cuts

    segment, token_position, member = request_layout(lengths, token_count)
    cosine, sine_part = rotation_tables(token_position)
    token_index = jnp.arange(token_count, dtype=jnp.int32)

    mixed, keys, values = [], [], []
    for c in range(CHUNKS):
        part = slice(c * size, (c + 1) * size)
        member_c = member[part]
        member_low = member_c.astype(jnp.bfloat16)

        def spread(low_part):
            return (member_low[:, :, None] * low_part[:, None, :]).reshape(size, flat_rank)

        x = gathered[c]
        low_next = jnp.einsum("td,jrd->tjr", x, req_down, preferred_element_type=jnp.float32)
        low_in = jnp.sum(jnp.where(member_c[:, :, None], low_next, 0.0), axis=1).astype(jnp.bfloat16)

        def projected(weight, low_part, up):
            return jnp.dot(x, weight, preferred_element_type=jnp.float32) + SCORE_SCALE * jnp.dot(
                spread(low_part), up, preferred_element_type=jnp.float32
            )

        query_lin = projected(query_weight, low_in[:, 0:rank], query_up)
        key_linear = projected(key_value_weight[0], low_in[:, rank : 2 * rank], key_up)
        value_linear = projected(key_value_weight[1], low_in[:, 2 * rank : 3 * rank], value_up)
        query_rows = apply_rotation(
            query_lin.reshape(size, query_local, HEAD_WIDTH), cosine[part], sine_part[part]
        ).astype(jnp.bfloat16)
        key_rows = apply_rotation(
            key_linear.reshape(size, keyval_local, HEAD_WIDTH), cosine[part], sine_part[part]
        ).astype(jnp.bfloat16)
        keys.append(key_rows)
        values.append(value_linear.astype(jnp.bfloat16).reshape(size, keyval_local, HEAD_WIDTH))
        reach = (c + 1) * size
        all_keys = jnp.concatenate(keys, axis=0)
        all_values = jnp.concatenate(values, axis=0)
        allowed = (segment[part][:, None] == segment[None, :reach]) & (
            token_index[None, :reach] <= token_index[part][:, None]
        )
        scores = (
            jnp.einsum(
                "hoyr,lor->oyhl",
                query_rows.reshape(size, keyval_local, query_group_width, HEAD_WIDTH),
                all_keys,
                preferred_element_type=jnp.float32,
            )
            * HEAD_WIDTH ** (-0.5)
        )
        scores = jnp.where(allowed[None, None], scores, NEG_FILL)
        maximum = jnp.max(scores, axis=-1, keepdims=True)
        exponent_part = jnp.exp(scores - maximum)
        weights = (exponent_part / jnp.sum(exponent_part, axis=-1, keepdims=True)).astype(jnp.bfloat16)
        attended = (
            jnp.einsum("kgts,skd->tkgd", weights, all_values, preferred_element_type=jnp.float32)
            .reshape(size, query_cols)
            .astype(jnp.bfloat16)
        )
        partial = jnp.dot(attended, output_weight, preferred_element_type=jnp.float32)
        base_output = line_reduce(partial, me, count)
        partial_low = jnp.dot(
            attended, out_down.T, preferred_element_type=jnp.float32
        ).reshape(size, request_count, rank)
        picked_out = jnp.sum(jnp.where(member_c[:, :, None], partial_low, 0.0), axis=1)
        low_out = small_sum(picked_out, count).astype(jnp.bfloat16)
        adapter_term = jnp.dot(spread(low_out), out_up, preferred_element_type=jnp.float32)
        mixed.append((base_output + SCORE_SCALE * adapter_term).astype(jnp.bfloat16))

    kv_cache = jnp.stack(
        [
            jnp.concatenate(keys, axis=0).reshape(token_count, keyval_cols),
            jnp.concatenate(values, axis=0).reshape(token_count, keyval_cols),
        ],
        axis=0,
    )
    return (jnp.concatenate(mixed, axis=0), kv_cache)


def solution(mesh):
    in_specs = (
        P(("groups", "adapter"), "tensor"),
        P(None, "tensor"),
        P(None, None, "tensor"),
        P("tensor", None),
        P(("groups", "adapter"), None, None),
        P(("groups", "adapter"), None, "tensor"),
        P(("groups", "adapter"), None, None, "tensor"),
        P(("groups", "adapter"), None, "tensor"),
        P(("groups", "adapter"), None, "tensor"),
        P("groups"),
        P(("groups", "adapter"), None),
        P(("groups", "adapter"), None),
    )
    out_specs = (P(("groups", "adapter"), "tensor"), P(None, ("groups", "adapter"), "tensor"))
    return jax.shard_map(local, mesh=mesh, in_specs=in_specs, out_specs=out_specs, check_vma=False)
```

time: 289 us -> 262 us (0.907)
  waiting for transfers between devices: 152 us -> 72 us
  starting transfers between devices: 18.1 us -> 71.4 us
  blocking collectives: 26.6 us -> 0 us
  matrix products: 31.6 us -> 53 us
  other arithmetic: 20.1 us -> 34.7 us
  between operations: 14.5 us -> 1.88 us
    reduce_scatter x1 -> x0, waiting for transfers between devices: 105 us -> none  [local(): lax.psum_scatter(jnp.dot(attended, output_weight, preferred_element_type=...]
    ppermute x0 -> x30, waiting for transfers between devices: none -> 68 us  [the longest x6 32.6 us: line_gather(): lax.ppermute(left, 'tensor', [(i, i - 1) for i in range(1, count - step +...]
    ppermute x0 -> x30, starting transfers between devices: none -> 60 us  [the longest x6 23.1 us: line_reduce(): lax.ppermute(to_right.astype(jnp.bfloat16), 'tensor', [(i, i + 1) for i i...]
    all_to_all x4 -> x2, waiting for transfers between devices: 36 us -> 3.94 us  [fetch(): lax.all_to_all(rows, 'adapter', split_axis=0, concat_axis=0, tiled=True)]
    psum x1 -> x0, blocking collectives: 18 us -> none  [local(): low_out = lax.psum(picked_out, 'tensor').astype(jnp.bfloat16)]
    convert_element_type x3 -> x12, other arithmetic: 0.16 us -> 12.7 us  [the longest x4 7.57 us: line_reduce(): to_right.astype(jnp.bfloat16)]
    dot_general x10 -> x20, matrix products: 24.7 us -> 35 us  [the longest x6 19.9 us: projected(): jnp.dot(x, weight, preferred_element_type=jnp.float32)]
    all_to_all x1 -> x0, blocking collectives: 8.55 us -> none  [local(): lax.all_to_all(select_rows(adapter_output_down), 'adapter', split_axis=0,...]
  transfers between devices with their start and end apart: 7 -> 33, of which waited for: 6 -> 11; matrix products, arithmetic and copies ran while one was open for 10% -> 40% of each run, Pallas kernels for 0% -> 0%
where the time goes in v1:
time: 262 us; the launch traced here: 260 us
  waiting for transfers between devices  72 us (27%)
  starting transfers between devices  71.4 us (27%)
  matrix products  53 us (20%)
  other arithmetic  34.7 us (13%)
  local copies, waits for them, and re-layouts  27.2 us (10%)
    ppermute x6, waiting for transfers between devices, line_gather(): lax.ppermute(left, 'tensor', [(i, i - 1) for i in range(1, count - step +...  32.6 us
    ppermute x6, starting transfers between devices, line_reduce(): lax.ppermute(to_right.astype(jnp.bfloat16), 'tensor', [(i, i + 1) for i i...  23.1 us
    dot_general x6, matrix products, projected(): jnp.dot(x, weight, preferred_element_type=jnp.float32)  19.9 us
    ppermute x6, waiting for transfers between devices, line_reduce(): lax.ppermute(to_right.astype(jnp.bfloat16), 'tensor', [(i, i + 1) for i i...  16 us
    ppermute x6, starting transfers between devices, line_gather(): lax.ppermute(right, 'tensor', [(i, i + 1) for i in range(step - 1, count...  14.5 us
    dot_general x2, matrix products, local(): jnp.dot(attended, output_weight, preferred_element_type=jnp.float32)  12 us
    ppermute x6, waiting for transfers between devices, line_reduce(): lax.ppermute(to_left.astype(jnp.bfloat16), 'tensor', [(i, i - 1) for i in...  11.9 us
    ppermute x6, starting transfers between devices, small_sum(): lax.ppermute(own, 'tensor', [(i, (i + k) % count) for i in range(count)])  8.27 us
  transfers between devices with their start and end apart: 33, of which 11 were waited for; matrix products, arithmetic and copies ran while one was open for 40% of the time, Pallas kernels for 0%

profile of v1, /device:TPU:0, one launch (start us, length us, event | category | flops | bytes accessed | tf_op | source)
XLA Modules:
  0.0 260.1 jit_solution(17517379132317387430)
XLA Ops:
  3.4 5.7 %collective-permute-start.1 = (bf16[256,1024]{1,0:T(8,128)(2,1)S(1)}, bf16[256,1024]{1,0:T(8,128)(2,1)}, u32[]{:S(2)}, u32[]{:S(2)}) collective-permute-start(bf16[256,1024]{1,0:T(8,128)(2,1)S(1)} %get-tuple-element.30), channel_id=1, source_target_pairs={{0,1},{1,2},{2,3},{4,5},{5,6},{6,7},{8,9},{9,10},{10,11},{12,13},{... | collective-permute-start | bytes 1572872 | tf_op jit(solution)/shard_map/ppermute | solution.py:53
  12.8 3.2 %all-to-all-start = ((s32[4,1,2]{2,1,0:T(1,128)}), s32[4,1,2]{2,1,0:T(1,128)S(1)}, u32[]{:S(2)}, u32[]{:S(2)}) async-start(s32[4,1,2]{2,1,0:T(1,128)} %bitcast.5), calls=%async_computation | async-start | bytes 4096 | tf_op jit(solution)/shard_map/all_to_all | solution.py:149
  21.9 1.6 gather_fusion.6
  23.5 1.6 gather_fusion.7
  29.0 3.5 %all-to-all-start.2 = ((bf16[4,2,16,3584]{3,2,1,0:T(8,128)(2,1)}), bf16[4,2,16,3584]{3,2,1,0:T(8,128)(2,1)S(1)}, u32[]{:S(2)}, u32[]{:S(2)}) async-start(bf16[4,2,16,3584]{3,2,1,0:T(8,128)(2,1)} %select_dynamic-update-slice_fusion.6), calls=%async_computation.2 | async-start | bytes 1835008 | tf_op jit(solution)/shard_map/all_to_all | solution.py:152
  32.5 5.2 %gather_fusion = bf16[8,48,4096]{2,1,0:T(8,128)(2,1)} fusion(bf16[16,48,4096]{2,1,0:T(8,128)(2,1)} %param.20, s32[1024]{0:T(1024)S(1)} %get-tuple-element.66), kind=kCustom, calls=%fused_computation.5 | custom fusion | bytes 6291488 | tf_op jit(solution)/shard_map/jit(_take)/gather | solution.py:156
  37.7 3.9 %broadcast_select_fusion = bf16[4,2,48,4096]{3,2,1,0:T(8,128)(2,1)} fusion(bf16[4,2,48,4096]{3,2,1,0:T(8,128)(2,1)} %bitcast.214, pred[4,2]{1,0:T(4,128)(4,1)S(1)} %copy.104), kind=kLoop, calls=%fused_computation.14 | loop fusion | flops 1572864 | bytes 6291464 | tf_op jit(solution)/shard_map/jit(_take)/select_n | solution.py:156
  41.6 3.9 %all-to-all-done.2 = bf16[4,2,16,3584]{3,2,1,0:T(8,128)(2,1)S(1)} async-done(((bf16[4,2,16,3584]{3,2,1,0:T(8,128)(2,1)}), bf16[4,2,16,3584]{3,2,1,0:T(8,128)(2,1)S(1)}, u32[]{:S(2)}, u32[]{:S(2)}) %all-to-all-start.2) | async-done | bytes 917536 | tf_op jit(solution)/shard_map/all_to_all | solution.py:152
  45.5 4.6 %all-to-all-start.1 = ((bf16[4,2,48,4096]{3,2,1,0:T(8,128)(2,1)}), bf16[4,2,48,4096]{3,2,1,0:T(8,128)(2,1)}, u32[]{:S(2)}, u32[]{:S(2)}) async-start(bf16[4,2,48,4096]{3,2,1,0:T(8,128)(2,1)} %broadcast_select_fusion), calls=%async_computation.1 | async-start | bytes 6291456 | tf_op jit(solution)/shard_map/all_to_all | solution.py:152
  55.4 15.5 %collective-permute-done.4 = bf16[256,1024]{1,0:T(8,128)(2,1)} collective-permute-done((bf16[256,1024]{1,0:T(8,128)(2,1)}, bf16[256,1024]{1,0:T(8,128)(2,1)}, u32[]{:S(2)}, u32[]{:S(2)}) %collective-permute-start.4) | collective-permute-done | bytes 524320 | tf_op jit(solution)/shard_map/ppermute | solution.py:54
  70.8 3.7 %collective-permute-start.16 = (bf16[256,1024]{1,0:T(8,128)(2,1)}, bf16[256,1024]{1,0:T(8,128)(2,1)S(1)}, u32[]{:S(2)}, u32[]{:S(2)}) collective-permute-start(bf16[256,1024]{1,0:T(8,128)(2,1)} %get-tuple-element.5), channel_id=1, source_target_pairs={{0,1},{1,2},{2,3},{4,5},{5,6},{6,7},{8,9},{9,10},{10,11},{12,13},{... | collective-permute-start | bytes 1572872 | tf_op jit(solution)/shard_map/ppermute | solution.py:53
  77.9 7.5 %collective-permute-done.16 = bf16[256,1024]{1,0:T(8,128)(2,1)S(1)} collective-permute-done((bf16[256,1024]{1,0:T(8,128)(2,1)}, bf16[256,1024]{1,0:T(8,128)(2,1)S(1)}, u32[]{:S(2)}, u32[]{:S(2)}) %collective-permute-start.16) | collective-permute-done | bytes 524320 | tf_op jit(solution)/shard_map/ppermute | solution.py:53
  86.9 4.6 %collective-permute-done.15 = bf16[256,1024]{1,0:T(8,128)(2,1)S(1)} collective-permute-done((bf16[256,1024]{1,0:T(8,128)(2,1)}, bf16[256,1024]{1,0:T(8,128)(2,1)S(1)}, u32[]{:S(2)}, u32[]{:S(2)}) %collective-permute-start.15) | collective-permute-done | bytes 524320 | tf_op jit(solution)/shard_map/ppermute | solution.py:54
  92.8 2.1 select_dynamic-update-slice_fusion.5
  94.8 2.1 select_dynamic-update-slice_fusion.4
  96.9 5.8 %collective-permute-done.5 = bf16[256,1024]{1,0:T(8,128)(2,1)S(1)} collective-permute-done((bf16[256,1024]{1,0:T(8,128)(2,1)}, bf16[256,1024]{1,0:T(8,128)(2,1)S(1)}, u32[]{:S(2)}, u32[]{:S(2)}) %collective-permute-start.5) | collective-permute-done | bytes 524320 | tf_op jit(solution)/shard_map/ppermute | solution.py:54
  105.2 6.8 %collective-permute-done.19 = bf16[256,1024]{1,0:T(8,128)(2,1)} collective-permute-done((bf16[256,1024]{1,0:T(8,128)(2,1)S(1)}, bf16[256,1024]{1,0:T(8,128)(2,1)}, u32[]{:S(2)}, u32[]{:S(2)}) %collective-permute-start.19) | collective-permute-done | bytes 524320 | tf_op jit(solution)/shard_map/ppermute | solution.py:54
  113.5 2.5 gather_fusion.1
  116.1 3.1 %fusion.64 = bf16[256,48]{0,1:T(8,128)(2,1)S(1)} fusion(bf16[256,4096]{1,0:T(8,128)(2,1)} %select_dynamic-update-slice_fusion.3, bf16[4,48,4096]{2,1,0:T(8,128)(2,1)S(1)} %gather_fusion.1, pred[4]{0:T(512)(128)(4,1)S(1)} %copy-done.29, pred[256,4]{0,1:T(4,128)(4,1)S(1)} %copy-done.31), kind=kOutput, calls=%fused_computation.72 | convolution fusion | flops 403525632 | bytes 3695620 | tf_op jit(solution)/shard_map/td,jrd->tjr/dot_general | solution.py:190
  119.7 2.6 fusion.52
  122.3 2.6 %fusion.39 = f32[256,256]{0,1:T(8,128)S(1)} fusion(f32[256,256]{0,1:T(8,128)S(1)} %fusion.46, bf16[256,4096]{1,0:T(8,128)(2,1)} %select_dynamic-update-slice_fusion.3, bf16[2,4096,256]{2,1,0:T(8,128)(2,1)S(1)} %copy-done.35), kind=kOutput, calls=%fused_computation.57 | convolution fusion | flops 536936448 | bytes 4718592 | tf_op jit(solution)/shard_map/dot_general | solution.py:194
  125.5 6.3 %fusion.29 = f32[32,8,8,128]{3,1,2,0:T(8,128)S(1)} fusion(f32[256,1024]{1,0:T(8,128)S(1)} %fusion.27, bf16[256,4096]{1,0:T(8,128)(2,1)} %select_dynamic-update-slice_fusion.3, bf16[4096,1024]{1,0:T(8,128)(2,1)} %param.17), kind=kOutput, calls=%fused_computation.51 | convolution fusion | flops 2147745792 | bytes 12582912 | tf_op jit(solution)/shard_map/dot_general | solution.py:194
  133.4 2.3 fusion.150
  135.7 1.9 convolution_convert_fusion
  137.7 6.1 %fusion.155 = f32[256,4096]{1,0:T(8,128)S(1)} fusion(bf16[256,1024]{0,1:T(8,128)(2,1)S(1)} %bitcast.221, bf16[1024,4096]{1,0:T(8,128)(2,1)} %param.19), kind=kOutput, calls=%fused_computation.234 | convolution fusion | flops 2147483648 | bytes 13107200 | tf_op jit(solution)/shard_map/dot_general | solution.py:233
  145.0 6.2 %collective-permute-start.6 = (bf16[256,1024]{1,0:T(8,128)(2,1)}, bf16[256,1024]{1,0:T(8,128)(2,1)}, u32[]{:S(2)}, u32[]{:S(2)}) collective-permute-start(bf16[256,1024]{1,0:T(8,128)(2,1)} %get-tuple-element.18), channel_id=1, source_target_pairs={{0,1},{4,5},{8,9},{12,13},{16,17},{20,21},{24,25},{28,29}} | collective-permute-start | bytes 1572872 | tf_op jit(solution)/shard_map/ppermute | solution.py:80
  156.2 1.6 fusion.49
  160.6 5.7 %fusion.28 = f32[32,8,8,128]{3,1,2,0:T(8,128)S(1)} fusion(f32[256,1024]{1,0:T(8,128)S(1)} %fusion.25, bf16[256,4096]{1,0:T(8,128)(2,1)S(1)} %select_dynamic-update-slice_fusion, bf16[4096,1024]{1,0:T(8,128)(2,1)} %param.17), kind=kOutput, calls=%fused_computation.49 | convolution fusion | flops 2147745792 | bytes 12582912 | tf_op jit(solution)/shard_map/dot_general | solution.py:194
  168.0 3.7 %fusion.149 = (f32[2,4,256]{2,1,0:T(4,128)S(1)}, f32[2,4,256,512]{2,3,1,0:T(8,128)}) fusion(pred[256,512]{0,1:T(8,128)(4,1)S(1)} %copy-done.22, bf16[256,2,128]{2,0,1:T(8,128)(2,1)S(1)} %maximum_convert_fusion.1, bf16[256,2,128]{2,0,1:T(8,128)(2,1)S(1)} %copy-done.16, bf16[256,2,4,64]{3,0,2,1:T(8,128)(2,1)S(1)} %bitcast.228, ...), kind=kOutput, calls=%fused_computation.232 | convolution fusion | flops 274203136 | bytes 5120000 | tf_op jit(solution)/shard_map/sub | solution.py:226
  171.6 2.6 %fusion.30 = bf16[2,128,4,256]{3,1,2,0:T(8,128)(2,1)S(1)} fusion(f32[2,4,256,512]{2,3,1,0:T(8,128)} %get-tuple-element.62, f32[2,4,256]{2,1,0:T(4,128)S(1)} %get-tuple-element.61, bf16[256,2,128]{0,2,1:T(8,128)(2,1)S(1)} %bitcast.238, bf16[256,2,128]{0,2,1:T(8,128)(2,1)S(1)} %bitcast.236), kind=kOutput, calls=%fused_computation.52 | convolution fusion | flops 271319040 | bytes 4988928 | tf_op jit(solution)/shard_map/kgts,skd->tkgd/dot_general | solution.py:229
  174.3 5.9 %fusion.156 = f32[256,4096]{1,0:T(8,128)S(1)} fusion(bf16[256,1024]{0,1:T(8,128)(2,1)S(1)} %bitcast.223, bf16[1024,4096]{1,0:T(8,128)(2,1)} %param.19), kind=kOutput, calls=%fused_computation.235 | convolution fusion | flops 2147483648 | bytes 13107200 | tf_op jit(solution)/shard_map/dot_general | solution.py:233
  183.5 2.3 add_convert_fusion.10
  187.9 7.1 %collective-permute-done.21 = bf16[256,1024]{1,0:T(8,128)(2,1)S(1)} collective-permute-done((bf16[256,1024]{1,0:T(8,128)(2,1)S(1)}, bf16[256,1024]{1,0:T(8,128)(2,1)S(1)}, u32[]{:S(2)}, u32[]{:S(2)}) %collective-permute-start.21) | collective-permute-done | bytes 524320 | tf_op jit(solution)/shard_map/ppermute | solution.py:80
  196.0 5.2 %collective-permute-start.22 = (bf16[256,1024]{1,0:T(8,128)(2,1)}, bf16[256,1024]{1,0:T(8,128)(2,1)}, u32[]{:S(2)}, u32[]{:S(2)}) collective-permute-start(bf16[256,1024]{1,0:T(8,128)(2,1)} %add_convert_fusion.4), channel_id=1, source_target_pairs={{0,1},{1,2},{4,5},{5,6},{8,9},{9,10},{12,13},{13,14},{16,17},{17,1... | collective-permute-start | bytes 1572872 | tf_op jit(solution)/shard_map/ppermute | solution.py:80
  201.7 4.6 %collective-permute-done.7 = bf16[256,1024]{1,0:T(8,128)(2,1)S(1)} collective-permute-done((bf16[256,1024]{1,0:T(8,128)(2,1)}, bf16[256,1024]{1,0:T(8,128)(2,1)S(1)}, u32[]{:S(2)}, u32[]{:S(2)}) %collective-permute-start.7) | collective-permute-done | bytes 524320 | tf_op jit(solution)/shard_map/ppermute | solution.py:80
  207.1 2.0 add_convert_fusion.9
  210.7 4.2 %collective-permute-done.22 = bf16[256,1024]{1,0:T(8,128)(2,1)} collective-permute-done((bf16[256,1024]{1,0:T(8,128)(2,1)}, bf16[256,1024]{1,0:T(8,128)(2,1)}, u32[]{:S(2)}, u32[]{:S(2)}) %collective-permute-start.22) | collective-permute-done | bytes 524320 | tf_op jit(solution)/shard_map/ppermute | solution.py:80
  214.9 2.2 add_convert_fusion.3
  218.8 3.1 %collective-permute-start.27 = (f32[256,16]{0,1:T(8,128)S(1)}, f32[256,16]{0,1:T(8,128)S(1)}, u32[]{:S(2)}, u32[]{:S(2)}) collective-permute-start(f32[256,16]{0,1:T(8,128)S(1)} %fusion.68), channel_id=1, source_target_pairs={{0,1},{1,2},{2,3},{3,0},{4,5},{5,6},{6,7},{7,4},{8,9},{9,10},{10,1... | collective-permute-start | bytes 49160 | tf_op jit(solution)/shard_map/ppermute | solution.py:92
  221.9 2.2 collective-permute-start.28
  224.1 2.8 %collective-permute-start.29 = (f32[256,16]{0,1:T(8,128)S(1)}, f32[256,16]{0,1:T(8,128)S(1)}, u32[]{:S(2)}, u32[]{:S(2)}) collective-permute-start(f32[256,16]{0,1:T(8,128)S(1)} %fusion.68), channel_id=1, source_target_pairs={{0,3},{1,0},{2,1},{3,2},{4,7},{5,4},{6,5},{7,6},{8,11},{9,8},{10,9... | collective-permute-start | bytes 49160 | tf_op jit(solution)/shard_map/ppermute | solution.py:92
  226.9 2.2 collective-permute-start.8
  229.2 2.3 add_convert_fusion.7
  234.2 6.8 %collective-permute-start.23 = (bf16[256,1024]{1,0:T(8,128)(2,1)S(1)}, bf16[256,1024]{1,0:T(8,128)(2,1)}, u32[]{:S(2)}, u32[]{:S(2)}) collective-permute-start(bf16[256,1024]{1,0:T(8,128)(2,1)S(1)} %get-tuple-element.20), channel_id=1, source_target_pairs={{0,1},{1,2},{2,3},{4,5},{5,6},{6,7},{8,9},{9,10},{10,11},{12,13},{... | collective-permute-start | bytes 1572872 | tf_op jit(solution)/shard_map/ppermute | solution.py:80
  243.3 6.5 %collective-permute-done.11 = bf16[256,1024]{1,0:T(8,128)(2,1)} collective-permute-done((bf16[256,1024]{1,0:T(8,128)(2,1)}, bf16[256,1024]{1,0:T(8,128)(2,1)}, u32[]{:S(2)}, u32[]{:S(2)}) %collective-permute-start.11) | collective-permute-done | bytes 524320 | tf_op jit(solution)/shard_map/ppermute | solution.py:83
  249.9 2.0 add_convert_fusion.6
  251.8 5.4 %collective-permute-done.26 = bf16[256,1024]{1,0:T(8,128)(2,1)} collective-permute-done((bf16[256,1024]{1,0:T(8,128)(2,1)S(1)}, bf16[256,1024]{1,0:T(8,128)(2,1)}, u32[]{:S(2)}, u32[]{:S(2)}) %collective-permute-start.26) | collective-permute-done | bytes 524320 | tf_op jit(solution)/shard_map/ppermute | solution.py:83
  257.2 1.9 add_convert_fusion
  (222 shorter events, 60.7 us)
Async XLA Ops:
  0.6 19.6 %copy-start = (bf16[16,16,1024]{2,1,0:T(8,128)(2,1)S(1)}, bf16[16,16,1024]{2,1,0:T(8,128)(2,1)}, u32[]{:S(2)}) copy-start(bf16[16,16,1024]{2,1,0:T(8,128)(2,1)} %param.21) | copy-start | bytes 1572868
  0.7 15.3 %copy-start.39 = (s32[1,4]{1,0:T(1,128)S(1)}, s32[1,4]{1,0:T(1,128)}, u32[]{:S(2)}) copy-start(s32[1,4]{1,0:T(1,128)} %param.27) | copy-start | bytes 52
  0.7 16.2 %copy-start.21 = (bf16[16,2,16,256]{3,2,1,0:T(8,128)(2,1)S(1)}, bf16[16,2,16,256]{3,2,1,0:T(8,128)(2,1)}, u32[]{:S(2)}) copy-start(bf16[16,2,16,256]{3,2,1,0:T(8,128)(2,1)} %param.22) | copy-start | bytes 786436
  3.4 46.8 %collective-permute-start.1 = (bf16[256,1024]{1,0:T(8,128)(2,1)S(1)}, bf16[256,1024]{1,0:T(8,128)(2,1)}, u32[]{:S(2)}, u32[]{:S(2)}) collective-permute-start(bf16[256,1024]{1,0:T(8,128)(2,1)S(1)} %get-tuple-element.30), channel_id=1, source_target_pairs={{0,1},{1,2},{2,3},{4,5},{5,6},{6,7},{8,9},{9,10},{10,11},{12,13},{... | collective-permute-start | bytes 1572872 | tf_op jit(solution)/shard_map/ppermute | solution.py:53
  9.2 42.5 %collective-permute-start = (bf16[256,1024]{1,0:T(8,128)(2,1)S(1)}, bf16[256,1024]{1,0:T(8,128)(2,1)}, u32[]{:S(2)}, u32[]{:S(2)}) collective-permute-start(bf16[256,1024]{1,0:T(8,128)(2,1)S(1)} %get-tuple-element.30), channel_id=1, source_target_pairs={{1,0},{2,1},{3,2},{5,4},{6,5},{7,6},{9,8},{10,9},{11,10},{13,12},{... | collective-permute-start | bytes 1572872 | tf_op jit(solution)/shard_map/ppermute | solution.py:54
  12.8 6.9 %all-to-all-start = ((s32[4,1,2]{2,1,0:T(1,128)}), s32[4,1,2]{2,1,0:T(1,128)S(1)}, u32[]{:S(2)}, u32[]{:S(2)}) async-start(s32[4,1,2]{2,1,0:T(1,128)} %bitcast.5), calls=%async_computation | async-start | bytes 4096 | tf_op jit(solution)/shard_map/all_to_all | solution.py:149
  29.0 16.5 %all-to-all-start.2 = ((bf16[4,2,16,3584]{3,2,1,0:T(8,128)(2,1)}), bf16[4,2,16,3584]{3,2,1,0:T(8,128)(2,1)S(1)}, u32[]{:S(2)}, u32[]{:S(2)}) async-start(bf16[4,2,16,3584]{3,2,1,0:T(8,128)(2,1)} %select_dynamic-update-slice_fusion.6), calls=%async_computation.2 | async-start | bytes 1835008 | tf_op jit(solution)/shard_map/all_to_all | solution.py:152
  45.5 68.0 %all-to-all-start.1 = ((bf16[4,2,48,4096]{3,2,1,0:T(8,128)(2,1)}), bf16[4,2,48,4096]{3,2,1,0:T(8,128)(2,1)}, u32[]{:S(2)}, u32[]{:S(2)}) async-start(bf16[4,2,48,4096]{3,2,1,0:T(8,128)(2,1)} %broadcast_select_fusion), calls=%async_computation.1 | async-start | bytes 6291456 | tf_op jit(solution)/shard_map/all_to_all | solution.py:152
  50.2 5.1 %collective-permute-start.2 = (bf16[256,1024]{1,0:T(8,128)(2,1)}, bf16[256,1024]{1,0:T(8,128)(2,1)}, u32[]{:S(2)}, u32[]{:S(2)}) collective-permute-start(bf16[256,1024]{1,0:T(8,128)(2,1)} %collective-permute-done.1), channel_id=1, source_target_pairs={{1,2},{2,3},{5,6},{6,7},{9,10},{10,11},{13,14},{14,15},{17,18},{18... | collective-permute-start | bytes 1572872 | tf_op jit(solution)/shard_map/ppermute | solution.py:53
  51.7 19.1 %collective-permute-start.4 = (bf16[256,1024]{1,0:T(8,128)(2,1)}, bf16[256,1024]{1,0:T(8,128)(2,1)}, u32[]{:S(2)}, u32[]{:S(2)}) collective-permute-start(bf16[256,1024]{1,0:T(8,128)(2,1)} %collective-permute-done), channel_id=1, source_target_pairs={{1,0},{2,1},{5,4},{6,5},{9,8},{10,9},{13,12},{14,13},{17,16},{18,1... | collective-permute-start | bytes 1572872 | tf_op jit(solution)/shard_map/ppermute | solution.py:54
  53.1 23.4 %copy-start.29 = (pred[4]{0:T(512)(128)(4,1)S(1)}, pred[4]{0:T(512)(128)(4,1)}, u32[]{:S(2)}) copy-start(pred[4]{0:T(512)(128)(4,1)} %get-tuple-element.14) | copy-start | bytes 16
  70.8 14.6 %collective-permute-start.16 = (bf16[256,1024]{1,0:T(8,128)(2,1)}, bf16[256,1024]{1,0:T(8,128)(2,1)S(1)}, u32[]{:S(2)}, u32[]{:S(2)}) collective-permute-start(bf16[256,1024]{1,0:T(8,128)(2,1)} %get-tuple-element.5), channel_id=1, source_target_pairs={{0,1},{1,2},{2,3},{4,5},{5,6},{6,7},{8,9},{9,10},{10,11},{12,13},{... | collective-permute-start | bytes 1572872 | tf_op jit(solution)/shard_map/ppermute | solution.py:53
  74.5 17.0 %collective-permute-start.15 = (bf16[256,1024]{1,0:T(8,128)(2,1)}, bf16[256,1024]{1,0:T(8,128)(2,1)S(1)}, u32[]{:S(2)}, u32[]{:S(2)}) collective-permute-start(bf16[256,1024]{1,0:T(8,128)(2,1)} %get-tuple-element.5), channel_id=1, source_target_pairs={{1,0},{2,1},{3,2},{5,4},{6,5},{7,6},{9,8},{10,9},{11,10},{13,12},{... | collective-permute-start | bytes 1572872 | tf_op jit(solution)/shard_map/ppermute | solution.py:54
  75.8 17.0 %collective-permute-start.3 = (bf16[256,1024]{1,0:T(8,128)(2,1)}, bf16[256,1024]{1,0:T(8,128)(2,1)S(1)}, u32[]{:S(2)}, u32[]{:S(2)}) collective-permute-start(bf16[256,1024]{1,0:T(8,128)(2,1)} %collective-permute-done.2), channel_id=1, source_target_pairs={{2,3},{6,7},{10,11},{14,15},{18,19},{22,23},{26,27},{30,31}} | collective-permute-start | bytes 1572872 | tf_op jit(solution)/shard_map/ppermute | solution.py:53
  76.6 81.2 %copy-start.12 = (bf16[4,16,3584]{2,1,0:T(8,128)(2,1)}, bf16[4,16,3584]{2,1,0:T(8,128)(2,1)S(1)}, u32[]{:S(2)}) copy-start(bf16[4,16,3584]{2,1,0:T(8,128)(2,1)S(1)} %broadcast_select_fusion.4) | copy-start | bytes 1376260
  76.6 26.1 %collective-permute-start.5 = (bf16[256,1024]{1,0:T(8,128)(2,1)}, bf16[256,1024]{1,0:T(8,128)(2,1)S(1)}, u32[]{:S(2)}, u32[]{:S(2)}) collective-permute-start(bf16[256,1024]{1,0:T(8,128)(2,1)} %collective-permute-done.4), channel_id=1, source_target_pairs={{1,0},{5,4},{9,8},{13,12},{17,16},{21,20},{25,24},{29,28}} | collective-permute-start | bytes 1572872 | tf_op jit(solution)/shard_map/ppermute | solution.py:54
  85.4 18.3 %copy-start.17 = (bf16[256,1024]{1,0:T(8,128)(2,1)}, bf16[256,1024]{1,0:T(8,128)(2,1)S(1)}, u32[]{:S(2)}) copy-start(bf16[256,1024]{1,0:T(8,128)(2,1)S(1)} %collective-permute-done.16) | copy-start | bytes 1572868
  85.4 18.3 %collective-permute-start.17 = (bf16[256,1024]{1,0:T(8,128)(2,1)S(1)}, bf16[256,1024]{1,0:T(8,128)(2,1)}, u32[]{:S(2)}, u32[]{:S(2)}) collective-permute-start(bf16[256,1024]{1,0:T(8,128)(2,1)S(1)} %collective-permute-done.16), channel_id=1, source_target_pairs={{1,2},{2,3},{5,6},{6,7},{9,10},{10,11},{13,14},{14,15},{17,18},{18... | collective-permute-start | bytes 1572872 | tf_op jit(solution)/shard_map/ppermute | solution.py:53
  91.5 20.6 %collective-permute-start.19 = (bf16[256,1024]{1,0:T(8,128)(2,1)S(1)}, bf16[256,1024]{1,0:T(8,128)(2,1)}, u32[]{:S(2)}, u32[]{:S(2)}) collective-permute-start(bf16[256,1024]{1,0:T(8,128)(2,1)S(1)} %collective-permute-done.15), channel_id=1, source_target_pairs={{1,0},{2,1},{5,4},{6,5},{9,8},{10,9},{13,12},{14,13},{17,16},{18,1... | collective-permute-start | bytes 1572872 | tf_op jit(solution)/shard_map/ppermute | solution.py:54
  96.9 19.2 %copy-start.31 = (pred[256,4]{0,1:T(4,128)(4,1)S(1)}, pred[256,4]{0,1:T(4,128)(4,1)}, u32[]{:S(2)}) copy-start(pred[256,4]{0,1:T(4,128)(4,1)} %get-tuple-element.58) | copy-start | bytes 3076
  103.7 47.5 %collective-permute-start.18 = (bf16[256,1024]{1,0:T(8,128)(2,1)}, bf16[256,1024]{1,0:T(8,128)(2,1)}, u32[]{:S(2)}, u32[]{:S(2)}) collective-permute-start(bf16[256,1024]{1,0:T(8,128)(2,1)} %collective-permute-done.17), channel_id=1, source_target_pairs={{2,3},{6,7},{10,11},{14,15},{18,19},{22,23},{26,27},{30,31}} | collective-permute-start | bytes 1572872 | tf_op jit(solution)/shard_map/ppermute | solution.py:53
  112.0 40.7 %collective-permute-start.20 = (bf16[256,1024]{1,0:T(8,128)(2,1)}, bf16[256,1024]{1,0:T(8,128)(2,1)}, u32[]{:S(2)}, u32[]{:S(2)}) collective-permute-start(bf16[256,1024]{1,0:T(8,128)(2,1)} %collective-permute-done.19), channel_id=1, source_target_pairs={{1,0},{5,4},{9,8},{13,12},{17,16},{21,20},{25,24},{29,28}} | collective-permute-start | bytes 1572872 | tf_op jit(solution)/shard_map/ppermute | solution.py:54
  122.3 13.5 %copy-start.23 = (bf16[256,256]{0,1:T(8,128)(2,1)}, bf16[256,256]{0,1:T(8,128)(2,1)S(1)}, u32[]{:S(2)}) copy-start(bf16[256,256]{0,1:T(8,128)(2,1)S(1)} %fusion.52) | copy-start | bytes 393220
  137.7 13.5 %copy-start.20 = (bf16[256,1024]{1,0:T(8,128)(2,1)S(1)}, bf16[256,1024]{1,0:T(8,128)(2,1)}, u32[]{:S(2)}) copy-start(bf16[256,1024]{1,0:T(8,128)(2,1)} %copy-done.19) | copy-start | bytes 1572868
  145.0 38.6 %collective-permute-start.6 = (bf16[256,1024]{1,0:T(8,128)(2,1)}, bf16[256,1024]{1,0:T(8,128)(2,1)}, u32[]{:S(2)}, u32[]{:S(2)}) collective-permute-start(bf16[256,1024]{1,0:T(8,128)(2,1)} %get-tuple-element.18), channel_id=1, source_target_pairs={{0,1},{4,5},{8,9},{12,13},{16,17},{20,21},{24,25},{28,29}} | collective-permute-start | bytes 1572872 | tf_op jit(solution)/shard_map/ppermute | solution.py:80
  180.2 14.8 %copy-start.3 = (f32[256,4096]{1,0:T(8,128)}, f32[256,4096]{1,0:T(8,128)S(1)}, u32[]{:S(2)}) copy-start(f32[256,4096]{1,0:T(8,128)S(1)} %fusion.156) | copy-start | bytes 12582916
  181.3 13.6 %collective-permute-start.21 = (bf16[256,1024]{1,0:T(8,128)(2,1)S(1)}, bf16[256,1024]{1,0:T(8,128)(2,1)S(1)}, u32[]{:S(2)}, u32[]{:S(2)}) collective-permute-start(bf16[256,1024]{1,0:T(8,128)(2,1)S(1)} %get-tuple-element.22), channel_id=1, source_target_pairs={{0,1},{4,5},{8,9},{12,13},{16,17},{20,21},{24,25},{28,29}} | collective-permute-start | bytes 1572872 | tf_op jit(solution)/shard_map/ppermute | solution.py:80
  182.7 18.6 %copy-start.11 = (bf16[2,128,4,256]{3,1,2,0:T(8,128)(2,1)S(1)}, bf16[2,128,4,256]{3,1,2,0:T(8,128)(2,1)}, u32[]{:S(2)}) copy-start(bf16[2,128,4,256]{3,1,2,0:T(8,128)(2,1)} %copy-done.10) | copy-start | bytes 1572868
  182.7 18.6 %copy-start.13 = (bf16[4,16,3584]{2,1,0:T(8,128)(2,1)S(1)}, bf16[4,16,3584]{2,1,0:T(8,128)(2,1)}, u32[]{:S(2)}) copy-start(bf16[4,16,3584]{2,1,0:T(8,128)(2,1)} %copy-done.12) | copy-start | bytes 1376260
  182.7 18.6 %copy-start.32 = (pred[256,4]{0,1:T(4,128)(4,1)S(1)}, pred[256,4]{0,1:T(4,128)(4,1)}, u32[]{:S(2)}) copy-start(pred[256,4]{0,1:T(4,128)(4,1)} %get-tuple-element.58) | copy-start | bytes 3076
  182.7 18.9 %collective-permute-start.9 = (bf16[256,1024]{1,0:T(8,128)(2,1)}, bf16[256,1024]{1,0:T(8,128)(2,1)S(1)}, u32[]{:S(2)}, u32[]{:S(2)}) collective-permute-start(bf16[256,1024]{1,0:T(8,128)(2,1)} %get-tuple-element.19), channel_id=1, source_target_pairs={{3,2},{7,6},{11,10},{15,14},{19,18},{23,22},{27,26},{31,30}} | collective-permute-start | bytes 1572872 | tf_op jit(solution)/shard_map/ppermute | solution.py:83
  185.9 20.5 %collective-permute-start.7 = (bf16[256,1024]{1,0:T(8,128)(2,1)}, bf16[256,1024]{1,0:T(8,128)(2,1)S(1)}, u32[]{:S(2)}, u32[]{:S(2)}) collective-permute-start(bf16[256,1024]{1,0:T(8,128)(2,1)} %add_convert_fusion.10), channel_id=1, source_target_pairs={{0,1},{1,2},{4,5},{5,6},{8,9},{9,10},{12,13},{13,14},{16,17},{17,1... | collective-permute-start | bytes 1572872 | tf_op jit(solution)/shard_map/ppermute | solution.py:80
  187.2 22.0 %collective-permute-start.24 = (bf16[256,1024]{1,0:T(8,128)(2,1)}, bf16[256,1024]{1,0:T(8,128)(2,1)S(1)}, u32[]{:S(2)}, u32[]{:S(2)}) collective-permute-start(bf16[256,1024]{1,0:T(8,128)(2,1)} %get-tuple-element.23), channel_id=1, source_target_pairs={{3,2},{7,6},{11,10},{15,14},{19,18},{23,22},{27,26},{31,30}} | collective-permute-start | bytes 1572872 | tf_op jit(solution)/shard_map/ppermute | solution.py:83
  196.0 19.0 %collective-permute-start.22 = (bf16[256,1024]{1,0:T(8,128)(2,1)}, bf16[256,1024]{1,0:T(8,128)(2,1)}, u32[]{:S(2)}, u32[]{:S(2)}) collective-permute-start(bf16[256,1024]{1,0:T(8,128)(2,1)} %add_convert_fusion.4), channel_id=1, source_target_pairs={{0,1},{1,2},{4,5},{5,6},{8,9},{9,10},{12,13},{13,14},{16,17},{17,1... | collective-permute-start | bytes 1572872 | tf_op jit(solution)/shard_map/ppermute | solution.py:80
  201.5 16.3 %collective-permute-start.12 = (f32[256,16]{0,1:T(8,128)S(1)}, f32[256,16]{0,1:T(8,128)S(1)}, u32[]{:S(2)}, u32[]{:S(2)}) collective-permute-start(f32[256,16]{0,1:T(8,128)S(1)} %fusion.67), channel_id=1, source_target_pairs={{0,1},{1,2},{2,3},{3,0},{4,5},{5,6},{6,7},{7,4},{8,9},{9,10},{10,1... | collective-permute-start | bytes 49160 | tf_op jit(solution)/shard_map/ppermute | solution.py:92
  201.6 16.2 %collective-permute-start.13 = (f32[256,16]{0,1:T(8,128)S(1)}, f32[256,16]{0,1:T(8,128)S(1)}, u32[]{:S(2)}, u32[]{:S(2)}) collective-permute-start(f32[256,16]{0,1:T(8,128)S(1)} %fusion.67), channel_id=1, source_target_pairs={{0,2},{1,3},{2,0},{3,1},{4,6},{5,7},{6,4},{7,5},{8,10},{9,11},{10,... | collective-permute-start | bytes 49160 | tf_op jit(solution)/shard_map/ppermute | solution.py:92
  207.1 10.7 %collective-permute-start.14 = (f32[256,16]{0,1:T(8,128)S(1)}, f32[256,16]{0,1:T(8,128)S(1)}, u32[]{:S(2)}, u32[]{:S(2)}) collective-permute-start(f32[256,16]{0,1:T(8,128)S(1)} %fusion.67), channel_id=1, source_target_pairs={{0,3},{1,0},{2,1},{3,2},{4,7},{5,4},{6,5},{7,6},{8,11},{9,8},{10,9... | collective-permute-start | bytes 49160 | tf_op jit(solution)/shard_map/ppermute | solution.py:92
  209.2 17.7 %collective-permute-start.10 = (bf16[256,1024]{1,0:T(8,128)(2,1)S(1)}, bf16[256,1024]{1,0:T(8,128)(2,1)}, u32[]{:S(2)}, u32[]{:S(2)}) collective-permute-start(bf16[256,1024]{1,0:T(8,128)(2,1)S(1)} %get-tuple-element.17), channel_id=1, source_target_pairs={{2,1},{3,2},{6,5},{7,6},{10,9},{11,10},{14,13},{15,14},{18,17},{19... | collective-permute-start | bytes 1572872 | tf_op jit(solution)/shard_map/ppermute | solution.py:83
  217.1 14.4 %collective-permute-start.25 = (bf16[256,1024]{1,0:T(8,128)(2,1)}, bf16[256,1024]{1,0:T(8,128)(2,1)S(1)}, u32[]{:S(2)}, u32[]{:S(2)}) collective-permute-start(bf16[256,1024]{1,0:T(8,128)(2,1)} %get-tuple-element.21), channel_id=1, source_target_pairs={{2,1},{3,2},{6,5},{7,6},{10,9},{11,10},{14,13},{15,14},{18,17},{19... | collective-permute-start | bytes 1572872 | tf_op jit(solution)/shard_map/ppermute | solution.py:83
  218.8 15.4 %collective-permute-start.27 = (f32[256,16]{0,1:T(8,128)S(1)}, f32[256,16]{0,1:T(8,128)S(1)}, u32[]{:S(2)}, u32[]{:S(2)}) collective-permute-start(f32[256,16]{0,1:T(8,128)S(1)} %fusion.68), channel_id=1, source_target_pairs={{0,1},{1,2},{2,3},{3,0},{4,5},{5,6},{6,7},{7,4},{8,9},{9,10},{10,1... | collective-permute-start | bytes 49160 | tf_op jit(solution)/shard_map/ppermute | solution.py:92
  221.9 19.0 %collective-permute-start.28 = (f32[256,16]{0,1:T(8,128)S(1)}, f32[256,16]{0,1:T(8,128)S(1)}, u32[]{:S(2)}, u32[]{:S(2)}) collective-permute-start(f32[256,16]{0,1:T(8,128)S(1)} %fusion.68), channel_id=1, source_target_pairs={{0,2},{1,3},{2,0},{3,1},{4,6},{5,7},{6,4},{7,5},{8,10},{9,11},{10,... | collective-permute-start | bytes 49160 | tf_op jit(solution)/shard_map/ppermute | solution.py:92
  224.1 19.2 %collective-permute-start.29 = (f32[256,16]{0,1:T(8,128)S(1)}, f32[256,16]{0,1:T(8,128)S(1)}, u32[]{:S(2)}, u32[]{:S(2)}) collective-permute-start(f32[256,16]{0,1:T(8,128)S(1)} %fusion.68), channel_id=1, source_target_pairs={{0,3},{1,0},{2,1},{3,2},{4,7},{5,4},{6,5},{7,6},{8,11},{9,8},{10,9... | collective-permute-start | bytes 49160 | tf_op jit(solution)/shard_map/ppermute | solution.py:92
  226.9 15.3 %copy-start.25 = (bf16[256,256]{0,1:T(8,128)(2,1)S(1)}, bf16[256,256]{0,1:T(8,128)(2,1)}, u32[]{:S(2)}) copy-start(bf16[256,256]{0,1:T(8,128)(2,1)} %copy-done.23) | copy-start | bytes 393220
  226.9 15.3 %copy-start.27 = (bf16[256,256]{0,1:T(8,128)(2,1)S(1)}, bf16[256,256]{0,1:T(8,128)(2,1)}, u32[]{:S(2)}) copy-start(bf16[256,256]{0,1:T(8,128)(2,1)} %fusion.49) | copy-start | bytes 393220
  226.9 16.4 %collective-permute-start.8 = (bf16[256,1024]{1,0:T(8,128)(2,1)S(1)}, bf16[256,1024]{1,0:T(8,128)(2,1)}, u32[]{:S(2)}, u32[]{:S(2)}) collective-permute-start(bf16[256,1024]{1,0:T(8,128)(2,1)S(1)} %get-tuple-element.16), channel_id=1, source_target_pairs={{0,1},{1,2},{2,3},{4,5},{5,6},{6,7},{8,9},{9,10},{10,11},{12,13},{... | collective-permute-start | bytes 1572872 | tf_op jit(solution)/shard_map/ppermute | solution.py:80
  231.5 18.3 %collective-permute-start.11 = (bf16[256,1024]{1,0:T(8,128)(2,1)}, bf16[256,1024]{1,0:T(8,128)(2,1)}, u32[]{:S(2)}, u32[]{:S(2)}) collective-permute-start(bf16[256,1024]{1,0:T(8,128)(2,1)} %add_convert_fusion.7), channel_id=1, source_target_pairs={{1,0},{2,1},{3,2},{5,4},{6,5},{7,6},{9,8},{10,9},{11,10},{13,12},{... | collective-permute-start | bytes 1572872 | tf_op jit(solution)/shard_map/ppermute | solution.py:83
  234.2 17.6 %collective-permute-start.23 = (bf16[256,1024]{1,0:T(8,128)(2,1)S(1)}, bf16[256,1024]{1,0:T(8,128)(2,1)}, u32[]{:S(2)}, u32[]{:S(2)}) collective-permute-start(bf16[256,1024]{1,0:T(8,128)(2,1)S(1)} %get-tuple-element.20), channel_id=1, source_target_pairs={{0,1},{1,2},{2,3},{4,5},{5,6},{6,7},{8,9},{9,10},{10,11},{12,13},{... | collective-permute-start | bytes 1572872 | tf_op jit(solution)/shard_map/ppermute | solution.py:80
  241.0 16.2 %collective-permute-start.26 = (bf16[256,1024]{1,0:T(8,128)(2,1)S(1)}, bf16[256,1024]{1,0:T(8,128)(2,1)}, u32[]{:S(2)}, u32[]{:S(2)}) collective-permute-start(bf16[256,1024]{1,0:T(8,128)(2,1)S(1)} %add_convert_fusion.1), channel_id=1, source_target_pairs={{1,0},{2,1},{3,2},{5,4},{6,5},{7,6},{9,8},{10,9},{11,10},{13,12},{... | collective-permute-start | bytes 1572872 | tf_op jit(solution)/shard_map/ppermute | solution.py:83
  (27 other events, 147.6 us)

commit v2 on v0

v2 whole, which is shorter than its diff:
```python
import functools
import jax
import jax.numpy as jnp
from jax import lax
from jax.experimental import pallas as pl
from jax.experimental.pallas import tpu as pltpu
from jax.sharding import PartitionSpec as P

HEAD_WIDTH = 128
CAP = 2
CHUNKS = 4
LANES = 128


SCORE_SCALE = 0.5
THETA = 500000.0
NEG_FILL = -1e30
MESH = pl.DeviceIdType.MESH


def rotation_tables(token_position):
    half_width = HEAD_WIDTH // 2
    exponent = jnp.arange(half_width).astype(jnp.float32) * (2.0 / HEAD_WIDTH)
    frequency = THETA ** (-exponent)
    angles = token_position.astype(jnp.float32)[:, None] * frequency[None, :]
    cosine, sine_part = jnp.cos(angles), jnp.sin(angles)
    return (
        jnp.concatenate([cosine, cosine], axis=1),
        jnp.concatenate([-sine_part, sine_part], axis=1),
    )


def layer_kernel(
    count, owners, rank, mine_x, wq_in, wkv_in, wo_in, down_in, small_in, cos_ref, sin_ref,
    mask_ref, seg_ref, seg_row, mixed_ref, kv_ref,
    xg, wq, wkv, wo, down, small, query, att, acc, rs_out, rs_in, low_out, low_in,
    ag_send, ag_recv, rs_send, rs_recv, lo_send, lo_recv, ad_send, ad_recv, here,
):
    me = lax.axis_index("tensor")
    home = lax.axis_index("adapter")
    tokens, width = mine_x.shape
    size = tokens // CHUNKS
    query_cols = wq.shape[1]
    keyval_cols = wkv.shape[2]
    slots = small.shape[0] * small.shape[1]
    group = query_cols // keyval_cols
    dot = functools.partial(jnp.dot, preferred_element_type=jnp.float32)

    def dot_t(a, b):
        return lax.dot_general(a, b, (((1,), (1,)), ((), ())), preferred_element_type=jnp.float32)

    barrier = pltpu.get_barrier_semaphore()
    for k in range(1, count):
        pl.semaphore_signal(
            barrier, inc=1, device_id={"tensor": lax.rem(me + k, count)}, device_id_type=MESH
        )
    for k in range(1, owners):
        pl.semaphore_signal(
            barrier, inc=1, device_id={"adapter": lax.rem(home + k, owners)}, device_id_type=MESH
        )
    pl.semaphore_wait(barrier, count - 1 + owners - 1)

    def rows(c):
        return pl.ds(c * size, size)

    def columns(j):
        return pl.ds(pl.multiple_of(j * width, width), width)

    def gather_copy(way, hop, c, receiving):
        source = me - hop if way == 0 else me + hop
        source = source if receiving else (source + 1 if way == 0 else source - 1)
        place = xg.at[rows(c), columns(source)]
        return pltpu.make_async_remote_copy(
            src_ref=mine_x.at[rows(c), :] if hop == 1 else place,
            dst_ref=place,
            send_sem=ag_send.at[way, hop - 1, c],
            recv_sem=ag_recv.at[way, hop - 1, c],
            device_id={"tensor": me + 1 if way == 0 else me - 1},
            device_id_type=MESH,
        )

    def sends_gather(way, hop):
        if way == 0:
            return jnp.logical_and(me >= hop - 1, me < count - 1)
        return jnp.logical_and(me <= count - hop, me > 0)

    def takes_gather(way, hop):
        return me >= hop if way == 0 else me <= count - 1 - hop

    def send_gather(c, hop):
        for way in range(2):
            @pl.when(sends_gather(way, hop))
            def _():
                gather_copy(way, hop, c, False).start()

    def take_gather(c, hop):
        for way in range(2):
            @pl.when(takes_gather(way, hop))
            def _():
                gather_copy(way, hop, c, True).wait_recv()
        if hop < count - 1:
            send_gather(c, hop + 1)

    def adapter_copy(k, kind):
        source, place = (down_in, down) if kind == 0 else (small_in, small)
        there = lax.rem(home + k, owners)
        if kind == 0:
            src, dst = source.at[there], place.at[:, home]
        else:
            src, dst = source.at[there], place.at[home]
        return pltpu.make_async_remote_copy(
            src_ref=src,
            dst_ref=dst,
            send_sem=ad_send.at[k - 1, kind],
            recv_sem=ad_recv.at[k - 1, kind],
            device_id={"adapter": there},
            device_id_type=MESH,
        )

    locals_ = [
        pltpu.make_async_copy(mine_x, xg.at[:, columns(me)], here.at[0]),
        pltpu.make_async_copy(down_in.at[home], down.at[:, home], here.at[1]),
        pltpu.make_async_copy(small_in.at[home], small.at[home], here.at[2]),
        pltpu.make_async_copy(wq_in, wq, here.at[3]),
        pltpu.make_async_copy(wkv_in, wkv, here.at[4]),
        pltpu.make_async_copy(wo_in, wo, here.at[5]),
    ]
    send_gather(0, 1)
    for k in range(1, owners):
        adapter_copy(k, 0).start()
        adapter_copy(k, 1).start()
    for copy in locals_:
        copy.start()
    send_gather(1, 1)
    for hop in range(1, count):
        take_gather(0, hop)
    for copy in locals_:
        copy.wait()
    for k in range(1, owners):
        adapter_copy(k, 0).wait_recv()
        adapter_copy(k, 1).wait_recv()

    ups = small.shape[2]
    at_query, at_key, at_value = 0, query_cols, query_cols + keyval_cols
    at_down = at_value + keyval_cols
    at_up = at_down + query_cols

    def small_rows(start, extent):
        return small[:, :, start : start + extent].reshape(slots, extent)

    def rotate(values, c):
        half = HEAD_WIDTH // 2
        swapped = jnp.concatenate([values[:, half:], values[:, :half]], axis=1)
        return values * cos_ref[rows(c), :] + swapped * sin_ref[rows(c), :]

    def low_part(c):
        low = dot_t(xg[rows(c), :], down[...].reshape(3 * slots, down.shape[3]))
        mask = mask_ref[rows(c), :]
        return [
            jnp.where(mask > 0, low[:, i * slots : (i + 1) * slots], 0.0).astype(jnp.bfloat16)
            for i in range(3)
        ]

    def query_part(c, low):
        for h in range(0, query_cols, 2 * HEAD_WIDTH):
            lin = dot(xg[rows(c), :], wq[:, h : h + 2 * HEAD_WIDTH]) + SCORE_SCALE * dot(
                low, small_rows(at_query + h, 2 * HEAD_WIDTH)
            )
            for i in range(2):
                piece = rotate(lin[:, i * HEAD_WIDTH : (i + 1) * HEAD_WIDTH], c)
                query[:, h + i * HEAD_WIDTH : h + (i + 1) * HEAD_WIDTH] = piece.astype(jnp.bfloat16)

    def keyval_part(c, low_key, low_value):
        key = dot(xg[rows(c), :], wkv[0]) + SCORE_SCALE * dot(
            low_key, small_rows(at_key, keyval_cols)
        )
        for h in range(0, keyval_cols, HEAD_WIDTH):
            kv_ref[0, rows(c), h : h + HEAD_WIDTH] = rotate(key[:, h : h + HEAD_WIDTH], c).astype(
                jnp.bfloat16
            )
        value = dot(xg[rows(c), :], wkv[1]) + SCORE_SCALE * dot(
            low_value, small_rows(at_value, keyval_cols)
        )
        kv_ref[1, rows(c), :] = value.astype(jnp.bfloat16)

    def attention_part(c, g):
        reach = (c + 1) * size
        t_index = c * size + lax.broadcasted_iota(jnp.int32, (size, reach), 0)
        s_index = lax.broadcasted_iota(jnp.int32, (size, reach), 1)
        allowed = jnp.logical_and(
            seg_ref[rows(c), :] == seg_row[:, :reach], s_index <= t_index
        )
        head = slice(g * HEAD_WIDTH, (g + 1) * HEAD_WIDTH)
        key = kv_ref[0, :reach, head]
        value = kv_ref[1, :reach, head]
        for i in range(group):
            spot = slice((g * group + i) * HEAD_WIDTH, (g * group + i + 1) * HEAD_WIDTH)
            scores = dot_t(query[:, spot], key) * HEAD_WIDTH ** (-0.5)
            scores = jnp.where(allowed, scores, NEG_FILL)
            grown = jnp.exp(scores - jnp.max(scores, axis=-1, keepdims=True))
            weights = (grown / jnp.sum(grown, axis=-1, keepdims=True)).astype(jnp.bfloat16)
            att[rows(c), spot] = dot(weights, value).astype(jnp.bfloat16)

    def reduce_copy(way, step, c):
        return pltpu.make_async_remote_copy(
            src_ref=rs_out.at[way, step - 1, c],
            dst_ref=rs_in.at[way, step - 1, c],
            send_sem=rs_send.at[way, step - 1, c],
            recv_sem=rs_recv.at[way, step - 1, c],
            device_id={"tensor": me + 1 if way == 0 else me - 1},
            device_id_type=MESH,
        )

    def sends_reduce(way, step):
        return me <= step - 1 if way == 0 else me >= count - step

    def has_before(way):
        return me >= 1 if way == 0 else me <= count - 2

    def reduce_step(c, step):
        for way in range(2):
            @pl.when(sends_reduce(way, step))
            def _():
                block = me + count - step if way == 0 else me - count + step
                acc[...] = dot(att[rows(c), :], wo[:, columns(block)])
                if step > 1:
                    @pl.when(has_before(way))
                    def _():
                        reduce_copy(way, step - 1, c).wait_recv()
                        acc[...] += rs_in[way, step - 2, c].astype(jnp.float32)
                rs_out[way, step - 1, c] = acc[...].astype(jnp.bfloat16)
                reduce_copy(way, step, c).start()

    def low_copy(k, c, receiving):
        place = lax.rem(me + count - k, count) if receiving else me
        return pltpu.make_async_remote_copy(
            src_ref=low_out.at[c],
            dst_ref=low_in.at[c, place],
            send_sem=lo_send.at[k - 1, c],
            recv_sem=lo_recv.at[k - 1, c],
            device_id={"tensor": lax.rem(me + k, count)},
            device_id_type=MESH,
        )

    per = LANES // rank
    packed_rows = size // per

    def low_send(c):
        part = dot_t(att[rows(c), :], small_rows(at_down, query_cols))
        part = jnp.where(mask_ref[rows(c), :] > 0, part, 0.0)
        total = part[:, 0:rank]
        for s in range(1, slots // rank):
            total = total + part[:, s * rank : (s + 1) * rank]
        packed = jnp.concatenate(
            [total[i * packed_rows : (i + 1) * packed_rows] for i in range(per)], axis=1
        )
        low_out[c] = packed
        low_in[c, me] = packed
        for k in range(1, count):
            low_copy(k, c, False).start()

    def finish(c):
        acc[...] = dot(att[rows(c), :], wo[:, columns(me)])
        for k in range(1, count):
            low_copy(k, c, True).wait_recv()
        packed = low_in[c, 0]
        for j in range(1, count):
            packed = packed + low_in[c, j]
        low = jnp.concatenate([packed[:, i * rank : (i + 1) * rank] for i in range(per)], axis=0)
        low = jnp.concatenate([low] * (slots // rank), axis=1)
        low = jnp.where(mask_ref[rows(c), :] > 0, low, 0.0).astype(jnp.bfloat16)
        acc[...] += SCORE_SCALE * dot(low, small_rows(at_up, width))
        for way in range(2):
            @pl.when(has_before(way))
            def _():
                reduce_copy(way, count - 1, c).wait_recv()
                acc[...] += rs_in[way, count - 2, c].astype(jnp.float32)
        mixed_ref[rows(c), :] = acc[...].astype(jnp.bfloat16)

    for c in range(CHUNKS):
        if c + 2 < CHUNKS:
            send_gather(c + 2, 1)
        lows = low_part(c)
        work = [
            lambda: keyval_part(c, lows[1], lows[2]),
            lambda: query_part(c, lows[0]),
        ] + [functools.partial(attention_part, c, g) for g in range(keyval_cols // HEAD_WIDTH)]
        for i in range(max(len(work), count)):
            hop = i + 1
            if hop < count:
                if c >= 1:
                    reduce_step(c - 1, hop)
                if c + 1 < CHUNKS:
                    take_gather(c + 1, hop)
            if i < len(work):
                work[i]()
        low_send(c)
        if c >= 1:
            finish(c - 1)
    for step in range(1, count):
        reduce_step(CHUNKS - 1, step)
    finish(CHUNKS - 1)

    for c in range(CHUNKS):
        for hop in range(1, count):
            for way in range(2):
                @pl.when(sends_gather(way, hop))
                def _():
                    gather_copy(way, hop, c, False).wait_send()

                @pl.when(sends_reduce(way, hop))
                def _():
                    reduce_copy(way, hop, c).wait_send()
            low_copy(hop, c, False).wait_send()
    for k in range(1, owners):
        adapter_copy(k, 0).wait_send()
        adapter_copy(k, 1).wait_send()


def local(
    normed_hidden,
    query_weight,
    key_value_weight,
    output_weight,
    adapter_down_rows,
    adapter_query_up,
    adapter_key_value_up,
    adapter_output_down,
    adapter_output_up,
    adapter_cache_row,
    request_adapter_index,
    request_token_length,
):
    token_count = normed_hidden.shape[0]
    slice_width = normed_hidden.shape[1]
    rank = adapter_query_up.shape[1]
    model_width = adapter_down_rows.shape[2]
    held_adapter_count = adapter_down_rows.shape[0]
    owners = lax.axis_size("adapter")
    count = lax.axis_size("tensor")
    query_cols = query_weight.shape[1]
    keyval_cols = key_value_weight.shape[2]
    size = token_count // CHUNKS

    request_ids = request_adapter_index[0]
    lengths = request_token_length[0]
    request_count = request_ids.shape[0]
    catalog = jnp.arange(adapter_cache_row.shape[0], dtype=jnp.int32)
    holder_rows = jnp.sum(
        jnp.where(request_ids[:, None] == catalog[None, :], adapter_cache_row[None, :], 0), axis=1
    )
    owner_index = holder_rows // held_adapter_count
    local_slot = holder_rows % held_adapter_count
    request_order = jnp.arange(request_count, dtype=jnp.int32)
    earlier = (owner_index[:, None] == owner_index[None, :]) & (
        request_order[None, :] < request_order[:, None]
    )
    rank_within = jnp.sum(earlier.astype(jnp.int32), axis=1)
    placed = owner_index * CAP + rank_within
    targets = jnp.arange(owners * CAP, dtype=jnp.int32)
    want_table = jnp.sum(
        jnp.where(placed[:, None] == targets[None, :], local_slot[:, None], 0), axis=0
    )
    picked = lax.all_to_all(
        want_table.reshape(owners, CAP), "adapter", split_axis=0, concat_axis=0, tiled=True
    )
    down = jnp.take(adapter_down_rows, picked, axis=0)
    down = down.reshape(owners, CAP, 3, rank, model_width).transpose(0, 2, 1, 3, 4)
    down = down.reshape(owners, 3, CAP * rank, model_width)
    small = jnp.concatenate(
        [
            jnp.take(adapter_query_up, picked, axis=0),
            jnp.take(adapter_key_value_up[:, 0], picked, axis=0),
            jnp.take(adapter_key_value_up[:, 1], picked, axis=0),
            jnp.take(adapter_output_down, picked, axis=0),
            jnp.take(adapter_output_up, picked, axis=0),
        ],
        axis=-1,
    )
    small_width = small.shape[-1]
    small = small.reshape(owners, CAP * rank, small_width)

    ending = jnp.cumsum(lengths)
    starting = ending - lengths
    token_index = jnp.arange(token_count, dtype=jnp.int32)
    segment = jnp.sum((token_index[:, None] >= ending[None, :]).astype(jnp.int32), axis=1)
    member = segment[:, None] == request_order[None, :]
    token_position = token_index - jnp.sum(jnp.where(member, starting[None, :], 0), axis=1)
    cosine, sine_part = rotation_tables(token_position)
    slot_of = jnp.sum(jnp.where(member, placed[None, :], 0), axis=1)
    slots = owners * CAP * rank
    mask = (slot_of[:, None] == (jnp.arange(slots, dtype=jnp.int32) // rank)[None, :]).astype(
        jnp.float32
    )

    any_spec = pl.BlockSpec(memory_space=pl.ANY)
    vmem = pl.BlockSpec(memory_space=pltpu.VMEM)
    packed = (size * rank // LANES, LANES)
    dma = pltpu.SemaphoreType.DMA
    mixed, kv_cache = pl.pallas_call(
        functools.partial(layer_kernel, count, owners, rank),
        out_shape=(
            jax.ShapeDtypeStruct((token_count, slice_width), jnp.bfloat16),
            jax.ShapeDtypeStruct((2, token_count, keyval_cols), jnp.bfloat16),
        ),
        in_specs=[any_spec] * 6 + [vmem] * 5,
        out_specs=(vmem, vmem),
        scratch_shapes=[
            pltpu.VMEM((token_count, model_width), jnp.bfloat16),
            pltpu.VMEM(query_weight.shape, jnp.bfloat16),
            pltpu.VMEM(key_value_weight.shape, jnp.bfloat16),
            pltpu.VMEM(output_weight.shape, jnp.bfloat16),
            pltpu.VMEM((3, owners, CAP * rank, model_width), jnp.bfloat16),
            pltpu.VMEM((owners, CAP * rank, small_width), jnp.bfloat16),
            pltpu.VMEM((size, query_cols), jnp.bfloat16),
            pltpu.VMEM((token_count, query_cols), jnp.bfloat16),
            pltpu.VMEM((size, slice_width), jnp.float32),
            pltpu.VMEM((2, count - 1, CHUNKS, size, slice_width), jnp.bfloat16),
            pltpu.VMEM((2, count - 1, CHUNKS, size, slice_width), jnp.bfloat16),
            pltpu.VMEM((CHUNKS,) + packed, jnp.float32),
            pltpu.VMEM((CHUNKS, count) + packed, jnp.float32),
            dma((2, count - 1, CHUNKS)),
            dma((2, count - 1, CHUNKS)),
            dma((2, count - 1, CHUNKS)),
            dma((2, count - 1, CHUNKS)),
            dma((count - 1, CHUNKS)),
            dma((count - 1, CHUNKS)),
            dma((owners - 1, 2)),
            dma((owners - 1, 2)),
            dma((6,)),
        ],
        compiler_params=pltpu.CompilerParams(
            collective_id=0, has_side_effects=True, vmem_limit_bytes=60 * 1024 * 1024
        ),
    )(
        normed_hidden, query_weight, key_value_weight, output_weight, down, small,
        cosine, sine_part, mask, segment[:, None], segment[None, :],
    )
    return (mixed, kv_cache)


def solution(mesh):
    in_specs = (
        P(("groups", "adapter"), "tensor"),
        P(None, "tensor"),
        P(None, None, "tensor"),
        P("tensor", None),
        P(("groups", "adapter"), None, None),
        P(("groups", "adapter"), None, "tensor"),
        P(("groups", "adapter"), None, None, "tensor"),
        P(("groups", "adapter"), None, "tensor"),
        P(("groups", "adapter"), None, "tensor"),
        P("groups"),
        P(("groups", "adapter"), None),
        P(("groups", "adapter"), None),
    )
    out_specs = (P(("groups", "adapter"), "tensor"), P(None, ("groups", "adapter"), "tensor"))
    return jax.shard_map(local, mesh=mesh, in_specs=in_specs, out_specs=out_specs, check_vma=False)
```

time: 289 us -> 175 us (0.61)
  the two profiles are of different devices: /device:TPU:0 before, /device:TPU:1 now
where the time goes in v2:
time: 175 us
  Pallas kernels  143 us (82%)
  local copies, waits for them, and re-layouts  16.2 us (9%)
  other arithmetic  10.2 us (6%)
  starting transfers between devices  4.26 us (2%)
    pallas_call x1, Pallas kernels, local(): pl.pallas_call(functools.partial(layer_kernel, count, owners, rank), out_...  143 us
    gather x1, local copies, waits for them, and re-layouts, local(): down = jnp.take(adapter_down_rows, picked, axis=0)  5.24 us
    unnamed x12, local copies, waits for them, and re-layouts  5.07 us
    all_to_all x1, starting transfers between devices, local(): lax.all_to_all(want_table.reshape(owners, CAP), 'adapter', split_axis=0,...  4.26 us
    select_n x3, other arithmetic, local(): down = jnp.take(adapter_down_rows, picked, axis=0)  4.02 us
  transfers between devices with their start and end apart: 1, of which 0 were waited for; matrix products, arithmetic and copies ran while one was open for 4% of the time, Pallas kernels for 0%

profile of v2, /device:TPU:1, one launch (start us, length us, event | category | flops | bytes accessed | tf_op | source)
XLA Modules:
  0.0 174.8 jit_solution(7388598848652168293)
XLA Ops:
  0.6 0.0 copy-start
  0.6 0.9 select_reduce_fusion.3
  1.6 0.2 convert_reduce_fusion.1
  1.8 0.1 select_reduce_fusion.2
  1.9 0.7 all_to_all.10
  2.5 4.3 %all-to-all-start = ((s32[4,1,2]{2,1,0:T(1,128)}), s32[4,1,2]{2,1,0:T(1,128)S(1)}, u32[]{:S(2)}, u32[]{:S(2)}) async-start(s32[4,1,2]{2,1,0:T(1,128)} %bitcast.1), calls=%async_computation | async-start | bytes 4096 | tf_op jit(solution)/shard_map/all_to_all | solution.py:364
  6.8 1.0 slice_bitcast_fusion
  7.8 0.8 reduce-window.4
  8.6 0.7 fusion.2
  9.3 0.1 convert_reduce_fusion
  9.4 0.0 copy-start.4
  9.4 0.1 select_reduce_fusion
  9.5 0.9 copy.78.seg_ref
  10.3 1.0 fusion
  11.3 0.8 compare_convert_fusion.mask_ref
  12.2 1.0 pad_maximum_fusion
  13.2 0.0 all-to-all-done
  13.2 0.1 copy.63
  13.3 0.1 copy.69
  13.4 0.1 reshape.224
  13.5 0.1 copy.66
  13.6 0.1 reshape.206
  13.7 0.1 copy.64
  13.8 5.2 %gather_fusion = bf16[8,48,4096]{2,1,0:T(8,128)(2,1)} fusion(bf16[16,48,4096]{2,1,0:T(8,128)(2,1)} %param.20, s32[1024]{0:T(1024)S(1)} %get-tuple-element.14), kind=kCustom, calls=%fused_computation.5 | custom fusion | bytes 6291488 | tf_op jit(solution)/shard_map/jit(_take)/gather | solution.py:367
  19.0 0.0 copy-done.4
  19.0 0.0 copy-start.2
  19.0 0.0 copy-start.3
  19.0 4.0 %copy_select_fusion = bf16[4,2,3,16,4096]{4,3,1,2,0:T(8,128)(2,1)} fusion(bf16[4,2,3,16,4096]{4,3,2,1,0:T(8,128)(2,1)} %bitcast.34, pred[4,2]{1,0:T(4,128)(4,1)S(1)} %copy.64), kind=kLoop, calls=%fused_computation.6 | loop fusion | flops 1572864 | bytes 6291464 | tf_op jit(solution)/shard_map/jit(_take)/select_n | solution.py:367
  23.0 0.0 copy-done
  23.0 0.6 gather_fusion.1
  23.6 0.1 select_dynamic-update-slice_fusion.2
  23.7 0.6 gather_fusion.2
  24.3 0.6 gather_fusion.3
  24.8 0.0 copy-done.2
  24.8 0.6 gather_fusion.4
  25.4 0.0 copy-done.3
  25.4 0.6 gather_fusion.5
  26.0 0.1 select_dynamic-update-slice_fusion.4
  26.1 0.1 select_dynamic-update-slice_fusion.3
  26.2 0.1 select_dynamic-update-slice_fusion.1
  26.3 0.1 select_dynamic-update-slice_fusion
  26.4 0.0 copy-start.1
  26.4 0.9 copy-done.1
  27.3 143.3 %shard_map.131 = (bf16[512,1024]{1,0:T(8,128)(2,1)}, bf16[2,512,256]{2,1,0:T(8,128)(2,1)}) custom-call(bf16[512,1024]{1,0:T(8,128)(2,1)} %mine_x.1, bf16[4096,1024]{1,0:T(8,128)(2,1)} %wq_in.1, bf16[2,4096,256]{2,1,0:T(8,128)(2,1)} %wkv_in.1, bf16[1024,4096]{1,0:T(8,128)(2,1)} %wo_in.1, bf16[4,3,32,4096]{3,2,1,0:T(8,128)(2,1)} %bitcast.35, ...), custom_call_target="tpu_custom_call" | custom-call | tf_op jit(solution)/shard_map/pallas_call | solution.py:400
  170.7 2.3 %copy.86 = bf16[512,1024]{1,0:T(8,128)(2,1)} copy(bf16[512,1024]{1,0:T(8,128)(2,1)} %get-tuple-element.19) | data formatting | bytes 2097152
  172.9 1.9 %copy.87 = bf16[2,512,256]{2,1,0:T(8,128)(2,1)} copy(bf16[2,512,256]{2,1,0:T(8,128)(2,1)} %get-tuple-element.20) | data formatting | bytes 1048576
  (9 shorter events, 0.1 us)
Async XLA Ops:
  0.6 22.4 %copy-start = (bf16[16,16,1024]{2,1,0:T(8,128)(2,1)S(1)}, bf16[16,16,1024]{2,1,0:T(8,128)(2,1)}, u32[]{:S(2)}) copy-start(bf16[16,16,1024]{2,1,0:T(8,128)(2,1)} %param.21) | copy-start | bytes 1572868
  2.5 10.7 %all-to-all-start = ((s32[4,1,2]{2,1,0:T(1,128)}), s32[4,1,2]{2,1,0:T(1,128)S(1)}, u32[]{:S(2)}, u32[]{:S(2)}) async-start(s32[4,1,2]{2,1,0:T(1,128)} %bitcast.1), calls=%async_computation | async-start | bytes 4096 | tf_op jit(solution)/shard_map/all_to_all | solution.py:364
  9.4 9.6 %copy-start.4 = (s32[512]{0:T(512)}, s32[512]{0:T(512)S(1)}, u32[]{:S(2)}) copy-start(s32[512]{0:T(512)S(1)} %convert_reduce_fusion) | copy-start | bytes 6148
  19.0 5.8 %copy-start.2 = (bf16[16,16,1024]{2,1,0:T(8,128)(2,1)S(1)}, bf16[16,16,1024]{2,1,0:T(8,128)(2,1)}, u32[]{:S(2)}) copy-start(bf16[16,16,1024]{2,1,0:T(8,128)(2,1)} %param.23) | copy-start | bytes 1572868
  19.0 6.4 %copy-start.3 = (bf16[16,16,1024]{2,1,0:T(8,128)(2,1)S(1)}, bf16[16,16,1024]{2,1,0:T(8,128)(2,1)}, u32[]{:S(2)}) copy-start(bf16[16,16,1024]{2,1,0:T(8,128)(2,1)} %param.24) | copy-start | bytes 1572868
  26.4 0.9 copy-start.1

commit v3 on v2

--- a/solution.py
+++ b/solution.py
@@ -33,8 +33,8 @@
 def layer_kernel(
     count, owners, rank, mine_x, wq_in, wkv_in, wo_in, down_in, small_in, cos_ref, sin_ref,
     mask_ref, seg_ref, seg_row, mixed_ref, kv_ref,
-    xg, wq, wkv, wo, down, small, query, att, acc, rs_out, rs_in, low_out, low_in,
-    ag_send, ag_recv, rs_send, rs_recv, lo_send, lo_recv, ad_send, ad_recv, here,
+    xg, wq, wkv, wo, down, small, query, base, att, acc, rs_out, rs_in, low_out, low_in, first_out, first_in,
+    ag_send, ag_recv, rs_send, rs_recv, lo_send, lo_recv, fi_send, fi_recv, ad_send, ad_recv, here,
 ):
     me = lax.axis_index("tensor")
     home = lax.axis_index("adapter")
@@ -132,15 +132,6 @@
     for copy in locals_:
         copy.start()
     send_gather(1, 1)
-    for hop in range(1, count):
-        take_gather(0, hop)
-    for copy in locals_:
-        copy.wait()
-    for k in range(1, owners):
-        adapter_copy(k, 0).wait_recv()
-        adapter_copy(k, 1).wait_recv()
-
-    ups = small.shape[2]
     at_query, at_key, at_value = 0, query_cols, query_cols + keyval_cols
     at_down = at_value + keyval_cols
     at_up = at_down + query_cols
@@ -153,35 +144,74 @@
         swapped = jnp.concatenate([values[:, half:], values[:, :half]], axis=1)
         return values * cos_ref[rows(c), :] + swapped * sin_ref[rows(c), :]
 
+    per = LANES // rank
+    packed_rows = size // per
+
+    def pack(part):
+        total = part[:, 0:rank]
+        for s in range(1, slots // rank):
+            total = total + part[:, s * rank : (s + 1) * rank]
+        return jnp.concatenate(
+            [total[i * packed_rows : (i + 1) * packed_rows] for i in range(per)], axis=1
+        )
+
+    def unpack(packed, c):
+        low = jnp.concatenate([packed[:, i * rank : (i + 1) * rank] for i in range(per)], axis=0)
+        low = jnp.concatenate([low] * (slots // rank), axis=1)
+        return jnp.where(mask_ref[rows(c), :] > 0, low, 0.0).astype(jnp.bfloat16)
+
+    def first_copy(k, receiving):
+        place = lax.rem(me + count - k, count) if receiving else me
+        return pltpu.make_async_remote_copy(
+            src_ref=first_out,
+            dst_ref=first_in.at[place],
+            send_sem=fi_send.at[k - 1],
+            recv_sem=fi_recv.at[k - 1],
+            device_id={"tensor": lax.rem(me + k, count)},
+            device_id_type=MESH,
+        )
+
+    def low_first():
+        maps = down[...].reshape(3 * slots, width)
+        for c in range(CHUNKS):
+            part = dot_t(xg[rows(c), columns(me)], maps)
+            mask = mask_ref[rows(c), :]
+            for i in range(3):
+                packed = pack(jnp.where(mask > 0, part[:, i * slots : (i + 1) * slots], 0.0))
+                first_out[c, i] = packed
+                first_in[me, c, i] = packed
+        for k in range(1, count):
+            first_copy(k, False).start()
+
     def low_part(c):
-        low = dot_t(xg[rows(c), :], down[...].reshape(3 * slots, down.shape[3]))
-        mask = mask_ref[rows(c), :]
-        return [
-            jnp.where(mask > 0, low[:, i * slots : (i + 1) * slots], 0.0).astype(jnp.bfloat16)
-            for i in range(3)
-        ]
-
-    def query_part(c, low):
+        lows = []
+        for i in range(3):
+            packed = first_in[0, c, i]
+            for j in range(1, count):
+                packed = packed + first_in[j, c, i]
+            lows.append(unpack(packed, c))
+        return lows
+
+    def base_part(c):
         for h in range(0, query_cols, 2 * HEAD_WIDTH):
-            lin = dot(xg[rows(c), :], wq[:, h : h + 2 * HEAD_WIDTH]) + SCORE_SCALE * dot(
-                low, small_rows(at_query + h, 2 * HEAD_WIDTH)
-            )
-            for i in range(2):
-                piece = rotate(lin[:, i * HEAD_WIDTH : (i + 1) * HEAD_WIDTH], c)
-                query[:, h + i * HEAD_WIDTH : h + (i + 1) * HEAD_WIDTH] = piece.astype(jnp.bfloat16)
-
-    def keyval_part(c, low_key, low_value):
-        key = dot(xg[rows(c), :], wkv[0]) + SCORE_SCALE * dot(
-            low_key, small_rows(at_key, keyval_cols)
-        )
+            base[:, h : h + 2 * HEAD_WIDTH] = dot(xg[rows(c), :], wq[:, h : h + 2 * HEAD_WIDTH])
+        for i in range(2):
+            start = query_cols + i * keyval_cols
+            base[:, start : start + keyval_cols] = dot(xg[rows(c), :], wkv[i])
+
+    def adapted(low, start, extent):
+        return base[:, start : start + extent] + SCORE_SCALE * dot(
+            low, small_rows(at_query + start, extent)
+        )
+
+    def rotary_part(c, lows):
+        for h in range(0, query_cols, HEAD_WIDTH):
+            piece = rotate(adapted(lows[0], h, HEAD_WIDTH), c)
+            query[:, h : h + HEAD_WIDTH] = piece.astype(jnp.bfloat16)
         for h in range(0, keyval_cols, HEAD_WIDTH):
-            kv_ref[0, rows(c), h : h + HEAD_WIDTH] = rotate(key[:, h : h + HEAD_WIDTH], c).astype(
-                jnp.bfloat16
-            )
-        value = dot(xg[rows(c), :], wkv[1]) + SCORE_SCALE * dot(
-            low_value, small_rows(at_value, keyval_cols)
-        )
-        kv_ref[1, rows(c), :] = value.astype(jnp.bfloat16)
+            piece = rotate(adapted(lows[1], at_key + h, HEAD_WIDTH), c)
+            kv_ref[0, rows(c), h : h + HEAD_WIDTH] = piece.astype(jnp.bfloat16)
+        kv_ref[1, rows(c), :] = adapted(lows[2], at_value, keyval_cols).astype(jnp.bfloat16)
 
     def attention_part(c, g):
         reach = (c + 1) * size
@@ -242,18 +272,9 @@
             device_id_type=MESH,
         )
 
-    per = LANES // rank
-    packed_rows = size // per
-
     def low_send(c):
         part = dot_t(att[rows(c), :], small_rows(at_down, query_cols))
-        part = jnp.where(mask_ref[rows(c), :] > 0, part, 0.0)
-        total = part[:, 0:rank]
-        for s in range(1, slots // rank):
-            total = total + part[:, s * rank : (s + 1) * rank]
-        packed = jnp.concatenate(
-            [total[i * packed_rows : (i + 1) * packed_rows] for i in range(per)], axis=1
-        )
+        packed = pack(jnp.where(mask_ref[rows(c), :] > 0, part, 0.0))
         low_out[c] = packed
         low_in[c, me] = packed
         for k in range(1, count):
@@ -266,9 +287,7 @@
         packed = low_in[c, 0]
         for j in range(1, count):
             packed = packed + low_in[c, j]
-        low = jnp.concatenate([packed[:, i * rank : (i + 1) * rank] for i in range(per)], axis=0)
-        low = jnp.concatenate([low] * (slots // rank), axis=1)
-        low = jnp.where(mask_ref[rows(c), :] > 0, low, 0.0).astype(jnp.bfloat16)
+        low = unpack(packed, c)
         acc[...] += SCORE_SCALE * dot(low, small_rows(at_up, width))
         for way in range(2):
             @pl.when(has_before(way))
@@ -277,30 +296,54 @@
                 acc[...] += rs_in[way, count - 2, c].astype(jnp.float32)
         mixed_ref[rows(c), :] = acc[...].astype(jnp.bfloat16)
 
+    for copy in locals_[:3]:
+        copy.wait()
+    for hop in range(1, count):
+        take_gather(0, hop)
+    if CHUNKS > 2:
+        send_gather(2, 1)
+    for k in range(1, owners):
+        adapter_copy(k, 0).wait_recv()
+        adapter_copy(k, 1).wait_recv()
+    low_first()
+    for copy in locals_[3:]:
+        copy.wait()
+    take_gather(1, 1)
+    base_part(0)
+    for hop in range(2, count - 1):
+        take_gather(1, hop)
+    for k in range(1, count):
+        first_copy(k, True).wait_recv()
+
     for c in range(CHUNKS):
-        if c + 2 < CHUNKS:
-            send_gather(c + 2, 1)
-        lows = low_part(c)
+        if c + 3 < CHUNKS:
+            send_gather(c + 3, 1)
         work = [
-            lambda: keyval_part(c, lows[1], lows[2]),
-            lambda: query_part(c, lows[0]),
+            (lambda: base_part(c)) if c else (lambda: None),
+            lambda: rotary_part(c, low_part(c)),
         ] + [functools.partial(attention_part, c, g) for g in range(keyval_cols // HEAD_WIDTH)]
         for i in range(max(len(work), count)):
             hop = i + 1
             if hop < count:
                 if c >= 1:
                     reduce_step(c - 1, hop)
-                if c + 1 < CHUNKS:
-                    take_gather(c + 1, hop)
+                if hop == 1 and c + 1 < CHUNKS:
+                    take_gather(c + 1, count - 1)
+                if hop > 1 and c + 2 < CHUNKS:
+                    take_gather(c + 2, hop - 1)
             if i < len(work):
                 work[i]()
         low_send(c)
-        if c >= 1:
-            finish(c - 1)
+        if c >= 2:
+            finish(c - 2)
     for step in range(1, count):
         reduce_step(CHUNKS - 1, step)
+        if step == 1:
+            finish(CHUNKS - 2)
     finish(CHUNKS - 1)
 
+    for k in range(1, count):
+        first_copy(k, False).wait_send()
     for c in range(CHUNKS):
         for hop in range(1, count):
             for way in range(2):
@@ -364,9 +407,12 @@
     picked = lax.all_to_all(
         want_table.reshape(owners, CAP), "adapter", split_axis=0, concat_axis=0, tiled=True
     )
-    down = jnp.take(adapter_down_rows, picked, axis=0)
-    down = down.reshape(owners, CAP, 3, rank, model_width).transpose(0, 2, 1, 3, 4)
-    down = down.reshape(owners, 3, CAP * rank, model_width)
+    own_down = lax.dynamic_slice_in_dim(
+        adapter_down_rows, lax.axis_index("tensor") * slice_width, slice_width, axis=2
+    )
+    down = jnp.take(own_down, picked, axis=0)
+    down = down.reshape(owners, CAP, 3, rank, slice_width).transpose(0, 2, 1, 3, 4)
+    down = down.reshape(owners, 3, CAP * rank, slice_width)
     small = jnp.concatenate(
         [
             jnp.take(adapter_query_up, picked, axis=0),
@@ -410,21 +456,26 @@
             pltpu.VMEM(query_weight.shape, jnp.bfloat16),
             pltpu.VMEM(key_value_weight.shape, jnp.bfloat16),
             pltpu.VMEM(output_weight.shape, jnp.bfloat16),
-            pltpu.VMEM((3, owners, CAP * rank, model_width), jnp.bfloat16),
+            pltpu.VMEM((3, owners, CAP * rank, slice_width), jnp.bfloat16),
             pltpu.VMEM((owners, CAP * rank, small_width), jnp.bfloat16),
             pltpu.VMEM((size, query_cols), jnp.bfloat16),
+            pltpu.VMEM((size, query_cols + 2 * keyval_cols), jnp.float32),
             pltpu.VMEM((token_count, query_cols), jnp.bfloat16),
             pltpu.VMEM((size, slice_width), jnp.float32),
             pltpu.VMEM((2, count - 1, CHUNKS, size, slice_width), jnp.bfloat16),
             pltpu.VMEM((2, count - 1, CHUNKS, size, slice_width), jnp.bfloat16),
             pltpu.VMEM((CHUNKS,) + packed, jnp.float32),
             pltpu.VMEM((CHUNKS, count) + packed, jnp.float32),
+            pltpu.VMEM((CHUNKS, 3) + packed, jnp.float32),
+            pltpu.VMEM((count, CHUNKS, 3) + packed, jnp.float32),
             dma((2, count - 1, CHUNKS)),
             dma((2, count - 1, CHUNKS)),
             dma((2, count - 1, CHUNKS)),
             dma((2, count - 1, CHUNKS)),
             dma((count - 1, CHUNKS)),
             dma((count - 1, CHUNKS)),
+            dma((count - 1,)),
+            dma((count - 1,)),
             dma((owners - 1, 2)),
             dma((owners - 1, 2)),
             dma((6,)),

time: 175 us -> 177 us (1.011)
  the two profiles are of different devices: /device:TPU:1 before, /device:TPU:0 now
where the time goes in v3:
time: 177 us
  Pallas kernels  147 us (83%)
  local copies, waits for them, and re-layouts  14.3 us (8%)
  other arithmetic  10.7 us (6%)
  starting transfers between devices  4.21 us (2%)
    pallas_call x1, Pallas kernels, local(): pl.pallas_call(functools.partial(layer_kernel, count, owners, rank), out_...  147 us
    all_to_all x1, starting transfers between devices, local(): lax.all_to_all(want_table.reshape(owners, CAP), 'adapter', split_axis=0,...  4.21 us
    unnamed x6, local copies, waits for them, and re-layouts  4.14 us
  transfers between devices with their start and end apart: 1, of which 0 were waited for; matrix products, arithmetic and copies ran while one was open for 5% of the time, Pallas kernels for 0%

profile of v3, /device:TPU:0, one launch (start us, length us, event | category | flops | bytes accessed | tf_op | source)
XLA Modules:
  0.0 176.8 jit_solution(7968121446697175955)
XLA Ops:
  0.6 0.0 copy-start
  0.6 0.9 select_reduce_fusion.3
  1.6 0.2 convert_reduce_fusion.1
  1.8 0.1 select_reduce_fusion.2
  1.9 0.7 all_to_all.10
  2.5 4.2 %all-to-all-start = ((s32[4,1,2]{2,1,0:T(1,128)}), s32[4,1,2]{2,1,0:T(1,128)S(1)}, u32[]{:S(2)}, u32[]{:S(2)}) async-start(s32[4,1,2]{2,1,0:T(1,128)} %bitcast.1), calls=%async_computation | async-start | bytes 4096 | tf_op jit(solution)/shard_map/all_to_all | solution.py:407
  6.7 1.0 slice_bitcast_fusion
  7.7 0.8 reduce-window.4
  8.6 0.7 fusion.2
  9.2 0.1 convert_reduce_fusion
  9.3 0.0 copy-start.1
  9.3 0.1 select_reduce_fusion
  9.4 0.9 copy.78.seg_ref
  10.3 1.0 fusion
  11.3 1.6 constant_dynamic-slice_fusion
  12.9 0.8 compare_convert_fusion.mask_ref
  13.7 1.0 pad_maximum_fusion
  14.7 0.0 all-to-all-done
  14.7 0.1 copy.63
  14.8 0.1 copy.66
  14.9 0.1 reshape.206
  15.0 0.1 copy.69
  15.1 0.1 reshape.224
  15.2 0.1 copy.64
  15.3 0.0 copy-done
  15.3 0.6 gather_fusion.1
  15.9 0.6 gather_fusion.2
  16.4 0.6 gather_fusion.3
  17.0 1.6 gather_fusion.4
  18.6 1.6 gather_fusion.5
  20.2 0.8 select_dynamic-update-slice_fusion.2
  21.0 0.6 gather_fusion
  21.7 1.1 copy_select_fusion
  22.7 0.7 select_dynamic-update-slice_fusion.4
  23.4 0.7 select_dynamic-update-slice_fusion.3
  24.1 0.8 select_dynamic-update-slice_fusion.1
  24.9 0.8 select_dynamic-update-slice_fusion
  25.8 0.0 copy-done.1
  25.8 146.9 %shard_map.131 = (bf16[512,1024]{1,0:T(8,128)(2,1)}, bf16[2,512,256]{2,1,0:T(8,128)(2,1)}) custom-call(bf16[512,1024]{1,0:T(8,128)(2,1)} %mine_x.1, bf16[4096,1024]{1,0:T(8,128)(2,1)} %wq_in.1, bf16[2,4096,256]{2,1,0:T(8,128)(2,1)} %wkv_in.1, bf16[1024,4096]{1,0:T(8,128)(2,1)} %wo_in.1, bf16[4,3,32,1024]{3,2,1,0:T(8,128)(2,1)} %bitcast.34, ...), custom_call_target="tpu_custom_call" | custom-call | tf_op jit(solution)/shard_map/pallas_call | solution.py:446
  172.7 2.3 %copy.86 = bf16[512,1024]{1,0:T(8,128)(2,1)} copy(bf16[512,1024]{1,0:T(8,128)(2,1)} %get-tuple-element.19) | data formatting | bytes 2097152
  175.0 1.9 %copy.87 = bf16[2,512,256]{2,1,0:T(8,128)(2,1)} copy(bf16[2,512,256]{2,1,0:T(8,128)(2,1)} %get-tuple-element.20) | data formatting | bytes 1048576
  (9 shorter events, 0.1 us)
Async XLA Ops:
  0.6 14.7 %copy-start = (bf16[16,16,1024]{2,1,0:T(8,128)(2,1)S(1)}, bf16[16,16,1024]{2,1,0:T(8,128)(2,1)}, u32[]{:S(2)}) copy-start(bf16[16,16,1024]{2,1,0:T(8,128)(2,1)} %param.21) | copy-start | bytes 1572868
  2.5 12.2 %all-to-all-start = ((s32[4,1,2]{2,1,0:T(1,128)}), s32[4,1,2]{2,1,0:T(1,128)S(1)}, u32[]{:S(2)}, u32[]{:S(2)}) async-start(s32[4,1,2]{2,1,0:T(1,128)} %bitcast.1), calls=%async_computation | async-start | bytes 4096 | tf_op jit(solution)/shard_map/all_to_all | solution.py:407
  9.3 16.5 %copy-start.1 = (s32[512]{0:T(512)}, s32[512]{0:T(512)S(1)}, u32[]{:S(2)}) copy-start(s32[512]{0:T(512)S(1)} %convert_reduce_fusion) | copy-start | bytes 6148
